TPU v7x, 32 devices: a whole 2x2x4 slice. The times are simulated.
32 devices in a mesh: row: 16 (over z, x, core), col: 2 (over y).
Axes of the slice: x: 2, y: 2, z: 4, core: 2. Of those that a mesh axis runs over, the one named last changes fastest.
Arguments:
- positions: float32 [3, 131072], P(None, ('row', 'col')), may hold values from 0 to 385, as said below
- atom_type: int32 [131072], P(('row', 'col')), may hold values from 0 to 5
- krylov: float32 [16, 131072], P(None, ('row', 'col')), may hold values from -6 to 6
- block_order: int32 [131072], P(('row', 'col')), may hold values from 0 to 4095, as said below
- type_width: float32 [6], replicated, may hold values from 0.5 to 2.5
- type_hard: float32 [6], replicated, may hold values from 1 to 4
- pair_rows: int32 [16, 2, 512], P('row', 'col'), may hold values from 0 to 63, as said below
- pair_cols: int32 [16, 2, 512], P('row', 'col'), may hold values from 0 to 511, as said below
- pair_count: int32 [16, 2], P('row', 'col'), may hold values from 1 to 512, as said below
Outputs:
- coulomb_response: float32 [16, 131072], P(None, ('row', 'col'))
Inputs may be any that keep to these rules, and one draw needn't show every extreme that they name: `positions`: global block g is a cell of a grid with coordinates (g // 64, (g // 32) % 2, g % 32); each atom of block g lies in the box of sides 44, 30 and 44 whose lowest corner is the cell's coordinates times 11, 5 and 11. `block_order`: within each device's shard of 4096 atoms, the entries are a permutation of 0 to 4095. `pair_rows`: in slots below pair_count the pairs (i, j) are distinct, have i <= j, and their grid cells differ by at most 2 along the first and third dimensions and at most 4 along the second; for device (r, c), pair_cols // 32 is r, r + 1 or r + 2 there. Other slots hold indices in range that are not used. `pair_cols`: see pair_rows. `pair_count`: some device's list is full.
All inputs are finite; a program needn't handle non-finite values.
Results may differ from a plain program's by a relative error of at most 0.00665.
Values may be sent and summed in bfloat16 or wider, within the bound.
A program may use at most 128 MiB of HBM per device.

v0:
```python
import math

import jax
import jax.numpy as jnp
from jax import lax
from jax.sharding import PartitionSpec as P

BLK = 128


SOFTENING = 0.5


def passed_along(value, axis, steps):
    count = lax.axis_size(axis)
    leading, last = (max(0, -steps), min(count, count - steps))
    return lax.ppermute(value, axis, [(source, source + steps) for source in range(leading, last)])


def kernel_tiles(left_geometry, right_geometry):
    offsets = left_geometry[:, 0:3, :, None] - right_geometry[:, 0:3, None, :]
    distance = jnp.sqrt(jnp.sum(offsets * offsets, axis=1) + SOFTENING * SOFTENING)
    spread = left_geometry[:, 3, :, None] ** 2 + right_geometry[:, 3, None, :] ** 2
    return (lax.erf(distance * lax.rsqrt(spread)) / distance).astype(jnp.bfloat16)


def table_lookup(table_values, atom_type):
    selector = (
        atom_type[None, :] == jnp.arange(table_values.shape[0], dtype=jnp.int32)[:, None]
    ).astype(jnp.float32)
    return jnp.sum(table_values[:, None] * selector, axis=0)


def to_blocks(panel):
    return panel.reshape(panel.shape[0], -1, BLK).transpose(1, 0, 2)


def reduce_columns(col_acc, vector_count):
    grouped = col_acc.transpose(1, 0, 2).reshape(vector_count, 3, -1)
    from_prior = passed_along(grouped[:, 1].astype(jnp.bfloat16), "row", 1).astype(jnp.float32)
    from_second = passed_along(grouped[:, 2].astype(jnp.bfloat16), "row", 2).astype(jnp.float32)
    return grouped[:, 0] + from_prior + from_second


def on_device(
    positions,
    atom_type,
    krylov,
    block_order,
    type_width,
    type_hard,
    pair_rows,
    pair_cols,
    pair_count,
):
    shard_atoms = positions.shape[1]
    shard_blocks = shard_atoms // BLK
    widths = table_lookup(type_width, atom_type)
    hardness = table_lookup(type_hard, atom_type)
    geometry = jnp.concatenate([positions, widths[None, :]], axis=0)[:, block_order]
    ordered = krylov[:, block_order]
    packed = jnp.concatenate([geometry, ordered], axis=0)
    row_packed = lax.all_gather(packed, "col", axis=1, tiled=True)
    packed_next = passed_along(packed, "row", -1)
    packed_after = passed_along(packed, "row", -2)
    col_packed = jnp.concatenate([packed, packed_next, packed_after], axis=1)
    row_geometry = row_packed[0:4]
    row_vectors = row_packed[4:].astype(jnp.bfloat16)
    col_geometry = col_packed[0:4]
    col_vectors = col_packed[4:].astype(jnp.bfloat16)
    row_geo_blocks = to_blocks(row_geometry)
    row_vec_blocks = to_blocks(row_vectors)
    col_geo_blocks = to_blocks(col_geometry)
    col_vec_blocks = to_blocks(col_vectors)
    row_block_total = row_geo_blocks.shape[0]
    col_block_total = col_geo_blocks.shape[0]
    vector_count = ordered.shape[0]
    row_index = lax.axis_index("row")
    col_index = lax.axis_index("col")
    col_devices = lax.axis_size("col")
    rows_list = pair_rows.reshape(-1)
    cols_list = pair_cols.reshape(-1)
    slot_total = rows_list.shape[0]
    live_count = pair_count.reshape(())
    row_global = row_index * (col_devices * shard_blocks) + rows_list
    col_global = (
        cols_list // shard_blocks * col_devices + col_index
    ) * shard_blocks + cols_list % shard_blocks
    cols_local = jnp.clip(
        (cols_list // shard_blocks - row_index) * shard_blocks + cols_list % shard_blocks,
        0,
        3 * shard_blocks - 1,
    )
    batch_rows = math.gcd(slot_total, 128)

    def pair_step(turn_index, partials):
        row_acc, col_acc = partials
        first_slot = turn_index * batch_rows
        left_block = lax.dynamic_slice_in_dim(rows_list, first_slot, batch_rows)
        right_block = lax.dynamic_slice_in_dim(cols_local, first_slot, batch_rows)
        left_global = lax.dynamic_slice_in_dim(row_global, first_slot, batch_rows)
        right_global = lax.dynamic_slice_in_dim(col_global, first_slot, batch_rows)
        alive_now = (first_slot + jnp.arange(batch_rows, dtype=jnp.int32) < live_count).astype(
            jnp.float32
        )
        tiles_now = kernel_tiles(row_geo_blocks[left_block], col_geo_blocks[right_block])
        forward = jnp.einsum(
            "pab,pvb->pva",
            tiles_now,
            col_vec_blocks[right_block],
            preferred_element_type=jnp.float32,
        )
        row_acc = row_acc.at[left_block].add(forward * alive_now[:, None, None])
        mirror = alive_now * (left_global != right_global).astype(jnp.float32)
        backward = jnp.einsum(
            "pab,pva->pvb",
            tiles_now,
            row_vec_blocks[left_block],
            preferred_element_type=jnp.float32,
        )
        col_acc = col_acc.at[right_block].add(backward * mirror[:, None, None])
        return (row_acc, col_acc)

    row_start = jnp.zeros((row_block_total, vector_count, BLK), jnp.float32)
    col_start = jnp.zeros((col_block_total, vector_count, BLK), jnp.float32)
    row_acc, col_acc = lax.fori_loop(0, slot_total // batch_rows, pair_step, (row_start, col_start))
    col_part = reduce_columns(col_acc, vector_count)
    row_flat = row_acc.transpose(1, 0, 2).reshape(vector_count, -1)
    row_part = lax.psum_scatter(
        row_flat.astype(jnp.bfloat16), "col", scatter_dimension=1, tiled=True
    ).astype(jnp.float32)
    blocked = row_part + col_part
    result = jnp.zeros((vector_count, shard_atoms), jnp.float32).at[:, block_order].set(blocked)
    return result + hardness[None, :] * krylov


def solution(mesh):
    placed = (
        P(None, ("row", "col")),
        P(("row", "col")),
        P(None, ("row", "col")),
        P(("row", "col")),
        P(),
        P(),
        P("row", "col", None),
        P("row", "col", None),
        P("row", "col"),
    )
    return jax.shard_map(
        on_device, mesh=mesh, in_specs=placed, out_specs=P(None, ("row", "col")), check_vma=False
    )
```

profile of v0, /device:TPU:0, one launch (start us, length us, event | category | flops | bytes accessed | tf_op | source)
XLA Modules:
  0.0 283.5 jit_solution(2274439413860454639)
XLA Ops:
  10.9 14.1 %gather_fusion.4 = f32[4096,4]{1,0:T(8,128)} fusion(f32[4,4096]{0,1:T(8,128)S(1)} %copy.66, s32[4096]{0:T(1024)S(1)} %get-tuple-element.241), kind=kCustom, calls=%fused_computation.4 | custom fusion | bytes 147456 | tf_op jit(solution)/shard_map/gather | solution.py:60
  27.8 14.1 %gather_fusion.5 = f32[4096,16]{1,0:T(8,128)} fusion(f32[16,4096]{0,1:T(8,128)S(1)} %copy.67, s32[4096]{0:T(1024)S(1)} %get-tuple-element.241), kind=kCustom, calls=%fused_computation.5 | custom fusion | bytes 540672 | tf_op jit(solution)/shard_map/gather | solution.py:61
  46.8 13.3 %all_gather.3 = f32[20,8192]{1,0:T(8,128)S(1)} all-gather(f32[20,4096]{1,0:T(8,128)S(1)} %pad_maximum_fusion.1), channel_id=1, replica_groups=mesh['row'=16,'col'=2] {'col'}, dimensions={1}, use_global_device_ids=true | all-gather | bytes 983040 | tf_op jit(solution)/shard_map/all_gather | solution.py:63
  63.5 182.4 %while.15 = (s32[]{:T(128)}, f32[64,16,128]{2,1,0:T(8,128)S(1)}, f32[96,16,128]{2,1,0:T(8,128)S(1)}, s32[512]{0:T(512)S(1)}, s32[512]{0:T(512)S(1)}, /*index=5*/...) while((s32[]{:T(128)}, f32[64,16,128]{2,1,0:T(8,128)S(1)}, ...), condition=%wide.region_5.6_spmd, body=%wide.region_1.5_spmd.sunk | while | flops 162565504 | bytes 44344676 | solution.py:126
  66.1 11.5 %multiply_reduce_fusion.2 = f32[128,128,128]{2,1,0:T(8,128)} fusion(f32[128,3,128]{2,1,0:T(4,128)S(1)} %bitcast.76, f32[128,3,128]{2,1,0:T(4,128)S(1)} %bitcast.77), kind=kLoop, calls=%fused_computation.9.clone.1 | loop fusion | flops 16777216 | bytes 8781824 | tf_op jit(solution)/shard_map/while/body/eval_jaxpr/reduce_sum | solution.py:22
  77.8 9.7 %fusion.26 = bf16[128,128,128]{2,1,0:T(8,128)(2,1)} fusion(f32[128,128,128]{2,1,0:T(8,128)} %multiply_reduce_fusion.2, f32[128,128]{1,0:T(8,128)S(1)} %bitcast.78, f32[128,128]{1,0:T(8,128)S(1)} %bitcast.79), kind=kLoop, calls=%fused_computation.11.clone.1 | loop fusion | flops 10485760 | bytes 12713984 | tf_op jit(solution)/shard_map/while/body/eval_jaxpr/convert_element_type | solution.py:24
  93.5 5.2 %scatter_fusion.1 = f32[96,16,128]{2,1,0:T(8,128)S(1)} fusion(f32[96,16,128]{2,1,0:T(8,128)S(1)} %get-tuple-element.345, s32[128]{0:T(128)S(1)} %get-tuple-element.324, f32[128,16,128]{2,1,0:T(8,128)S(1)} %convolution_multiply_fusion.5), kind=kCustom, calls=%fused_computation.7.clone.1 | custom fusion | flops 262144 | bytes 3146240 | tf_op jit(solution)/shard_map/while/body/eval_jaxpr/scatter-add | solution.py:121
  99.4 4.5 %convolution_multiply_fusion.4 = f32[128,16,128]{2,1,0:T(8,128)S(1)} fusion(bf16[128,16,128]{2,1,0:T(8,128)(2,1)S(1)} %gather_fusion, bf16[128,128,128]{2,1,0:T(8,128)(2,1)} %fusion.26, f32[128]{0:T(128)S(1)} %get-tuple-element.325), kind=kOutput, calls=%fused_computation.13.clone.1 | convolution fusion | flops 67371008 | bytes 5767680 | tf_op jit(solution)/shard_map/while/body/eval_jaxpr/pab,pvb->pva/dot_general | solution.py:107
  103.9 5.2 %scatter_fusion = f32[64,16,128]{2,1,0:T(8,128)S(1)} fusion(f32[64,16,128]{2,1,0:T(8,128)S(1)} %get-tuple-element.344, s32[128]{0:T(128)S(1)} %get-tuple-element.323, f32[128,16,128]{2,1,0:T(8,128)S(1)} %convolution_multiply_fusion.4), kind=kCustom, calls=%fused_computation.6.clone.1 | custom fusion | flops 262144 | bytes 3146240 | tf_op jit(solution)/shard_map/while/body/eval_jaxpr/scatter-add | solution.py:113
  111.7 11.5 %multiply_reduce_fusion.2 = f32[128,128,128]{2,1,0:T(8,128)} fusion(f32[128,3,128]{2,1,0:T(4,128)S(1)} %bitcast.76, f32[128,3,128]{2,1,0:T(4,128)S(1)} %bitcast.77), kind=kLoop, calls=%fused_computation.9.clone.1 | loop fusion | flops 16777216 | bytes 8781824 | tf_op jit(solution)/shard_map/while/body/eval_jaxpr/reduce_sum | solution.py:22
  123.4 9.7 %fusion.26 = bf16[128,128,128]{2,1,0:T(8,128)(2,1)} fusion(f32[128,128,128]{2,1,0:T(8,128)} %multiply_reduce_fusion.2, f32[128,128]{1,0:T(8,128)S(1)} %bitcast.78, f32[128,128]{1,0:T(8,128)S(1)} %bitcast.79), kind=kLoop, calls=%fused_computation.11.clone.1 | loop fusion | flops 10485760 | bytes 12713984 | tf_op jit(solution)/shard_map/while/body/eval_jaxpr/convert_element_type | solution.py:24
  139.1 5.2 %scatter_fusion.1 = f32[96,16,128]{2,1,0:T(8,128)S(1)} fusion(f32[96,16,128]{2,1,0:T(8,128)S(1)} %get-tuple-element.345, s32[128]{0:T(128)S(1)} %get-tuple-element.324, f32[128,16,128]{2,1,0:T(8,128)S(1)} %convolution_multiply_fusion.5), kind=kCustom, calls=%fused_computation.7.clone.1 | custom fusion | flops 262144 | bytes 3146240 | tf_op jit(solution)/shard_map/while/body/eval_jaxpr/scatter-add | solution.py:121
  145.0 4.5 %convolution_multiply_fusion.4 = f32[128,16,128]{2,1,0:T(8,128)S(1)} fusion(bf16[128,16,128]{2,1,0:T(8,128)(2,1)S(1)} %gather_fusion, bf16[128,128,128]{2,1,0:T(8,128)(2,1)} %fusion.26, f32[128]{0:T(128)S(1)} %get-tuple-element.325), kind=kOutput, calls=%fused_computation.13.clone.1 | convolution fusion | flops 67371008 | bytes 5767680 | tf_op jit(solution)/shard_map/while/body/eval_jaxpr/pab,pvb->pva/dot_general | solution.py:107
  149.5 5.2 %scatter_fusion = f32[64,16,128]{2,1,0:T(8,128)S(1)} fusion(f32[64,16,128]{2,1,0:T(8,128)S(1)} %get-tuple-element.344, s32[128]{0:T(128)S(1)} %get-tuple-element.323, f32[128,16,128]{2,1,0:T(8,128)S(1)} %convolution_multiply_fusion.4), kind=kCustom, calls=%fused_computation.6.clone.1 | custom fusion | flops 262144 | bytes 3146240 | tf_op jit(solution)/shard_map/while/body/eval_jaxpr/scatter-add | solution.py:113
  157.3 11.5 %multiply_reduce_fusion.2 = f32[128,128,128]{2,1,0:T(8,128)} fusion(f32[128,3,128]{2,1,0:T(4,128)S(1)} %bitcast.76, f32[128,3,128]{2,1,0:T(4,128)S(1)} %bitcast.77), kind=kLoop, calls=%fused_computation.9.clone.1 | loop fusion | flops 16777216 | bytes 8781824 | tf_op jit(solution)/shard_map/while/body/eval_jaxpr/reduce_sum | solution.py:22
  169.0 9.7 %fusion.26 = bf16[128,128,128]{2,1,0:T(8,128)(2,1)} fusion(f32[128,128,128]{2,1,0:T(8,128)} %multiply_reduce_fusion.2, f32[128,128]{1,0:T(8,128)S(1)} %bitcast.78, f32[128,128]{1,0:T(8,128)S(1)} %bitcast.79), kind=kLoop, calls=%fused_computation.11.clone.1 | loop fusion | flops 10485760 | bytes 12713984 | tf_op jit(solution)/shard_map/while/body/eval_jaxpr/convert_element_type | solution.py:24
  184.7 5.2 %scatter_fusion.1 = f32[96,16,128]{2,1,0:T(8,128)S(1)} fusion(f32[96,16,128]{2,1,0:T(8,128)S(1)} %get-tuple-element.345, s32[128]{0:T(128)S(1)} %get-tuple-element.324, f32[128,16,128]{2,1,0:T(8,128)S(1)} %convolution_multiply_fusion.5), kind=kCustom, calls=%fused_computation.7.clone.1 | custom fusion | flops 262144 | bytes 3146240 | tf_op jit(solution)/shard_map/while/body/eval_jaxpr/scatter-add | solution.py:121
  195.1 5.2 %scatter_fusion = f32[64,16,128]{2,1,0:T(8,128)S(1)} fusion(f32[64,16,128]{2,1,0:T(8,128)S(1)} %get-tuple-element.344, s32[128]{0:T(128)S(1)} %get-tuple-element.323, f32[128,16,128]{2,1,0:T(8,128)S(1)} %convolution_multiply_fusion.4), kind=kCustom, calls=%fused_computation.6.clone.1 | custom fusion | flops 262144 | bytes 3146240 | tf_op jit(solution)/shard_map/while/body/eval_jaxpr/scatter-add | solution.py:113
  202.9 11.5 %multiply_reduce_fusion.2 = f32[128,128,128]{2,1,0:T(8,128)} fusion(f32[128,3,128]{2,1,0:T(4,128)S(1)} %bitcast.76, f32[128,3,128]{2,1,0:T(4,128)S(1)} %bitcast.77), kind=kLoop, calls=%fused_computation.9.clone.1 | loop fusion | flops 16777216 | bytes 8781824 | tf_op jit(solution)/shard_map/while/body/eval_jaxpr/reduce_sum | solution.py:22
  214.6 9.7 %fusion.26 = bf16[128,128,128]{2,1,0:T(8,128)(2,1)} fusion(f32[128,128,128]{2,1,0:T(8,128)} %multiply_reduce_fusion.2, f32[128,128]{1,0:T(8,128)S(1)} %bitcast.78, f32[128,128]{1,0:T(8,128)S(1)} %bitcast.79), kind=kLoop, calls=%fused_computation.11.clone.1 | loop fusion | flops 10485760 | bytes 12713984 | tf_op jit(solution)/shard_map/while/body/eval_jaxpr/convert_element_type | solution.py:24
  230.3 5.2 %scatter_fusion.1 = f32[96,16,128]{2,1,0:T(8,128)S(1)} fusion(f32[96,16,128]{2,1,0:T(8,128)S(1)} %get-tuple-element.345, s32[128]{0:T(128)S(1)} %get-tuple-element.324, f32[128,16,128]{2,1,0:T(8,128)S(1)} %convolution_multiply_fusion.5), kind=kCustom, calls=%fused_computation.7.clone.1 | custom fusion | flops 262144 | bytes 3146240 | tf_op jit(solution)/shard_map/while/body/eval_jaxpr/scatter-add | solution.py:121
  240.7 5.2 %scatter_fusion = f32[64,16,128]{2,1,0:T(8,128)S(1)} fusion(f32[64,16,128]{2,1,0:T(8,128)S(1)} %get-tuple-element.344, s32[128]{0:T(128)S(1)} %get-tuple-element.323, f32[128,16,128]{2,1,0:T(8,128)S(1)} %convolution_multiply_fusion.4), kind=kCustom, calls=%fused_computation.6.clone.1 | custom fusion | flops 262144 | bytes 3146240 | tf_op jit(solution)/shard_map/while/body/eval_jaxpr/scatter-add | solution.py:113
  249.1 4.9 %collective-permute-start.3 = (bf16[16,4096]{1,0:T(8,128)(2,1)S(1)}, bf16[16,4096]{1,0:T(8,128)(2,1)S(1)}, u32[]{:S(2)}, u32[]{:S(2)}) collective-permute-start(bf16[16,4096]{1,0:T(8,128)(2,1)S(1)} %get-tuple-element.240), channel_id=1, source_target_pairs={{0,4},{2,6},{4,8},{6,10},{8,12},{10,14},{12,16},{14,18},{16,20},{1... | collective-permute-start | bytes 393224 | tf_op jit(solution)/shard_map/ppermute | solution.py:17
  263.9 11.4 %scatter_custom_fusion.2 = f32[16,4096]{0,1:T(8,128)S(1)} fusion(s32[4096]{0:T(1024)} %get-tuple-element.242, f32[4096,16]{1,0:T(8,128)} %copy.78, f32[]{:T(128)} %constant.102.clone.1), kind=kCustom, calls=%fused_computation.23 | custom fusion | bytes 262656 | tf_op jit(solution)/shard_map/scatter | solution.py:133
  (131 shorter events, 76.2 us)
Async XLA Ops:
  6.5 254.5 %reduce-scatter.2.cloned.1.call-start = ((), (), s32[]{:S(2)}) async-start(), calls=%async_computation.1 | async-start | bytes 393216 | tf_op jit(solution)/shard_map/reduce_scatter | solution.py:129
  10.2 17.0 %copy-start.2 = (f32[16,4096]{1,0:T(8,128)S(1)}, f32[16,4096]{1,0:T(8,128)}, u32[]{:S(2)}) copy-start(f32[16,4096]{1,0:T(8,128)} %param.13) | copy-start | bytes 786436
  41.9 18.8 %copy-start.5 = (s32[1,1,512]{2,1,0:T(1,128)S(1)}, s32[1,1,512]{2,1,0:T(1,128)}, u32[]{:S(2)}) copy-start(s32[1,1,512]{2,1,0:T(1,128)} %param.17) | copy-start | bytes 6148
  41.9 18.8 %copy-start.9 = (s32[1,1,512]{2,1,0:T(1,128)S(1)}, s32[1,1,512]{2,1,0:T(1,128)}, u32[]{:S(2)}) copy-start(s32[1,1,512]{2,1,0:T(1,128)} %param.18) | copy-start | bytes 6148
  44.2 17.2 %collective-permute-start = (f32[20,4096]{1,0:T(8,128)S(1)}, f32[20,4096]{1,0:T(8,128)S(1)}, u32[]{:S(2)}, u32[]{:S(2)}) collective-permute-start(f32[20,4096]{1,0:T(8,128)S(1)} %pad_maximum_fusion.1), channel_id=1, source_target_pairs={{2,0},{4,2},{6,4},{8,6},{10,8},{12,10},{14,12},{16,14},{18,16},{20... | collective-permute-start | bytes 983048 | tf_op jit(solution)/shard_map/ppermute | solution.py:17
  45.5 17.7 %collective-permute-start.1 = (f32[20,4096]{1,0:T(8,128)S(1)}, f32[20,4096]{1,0:T(8,128)S(1)}, u32[]{:S(2)}, u32[]{:S(2)}) collective-permute-start(f32[20,4096]{1,0:T(8,128)S(1)} %pad_maximum_fusion.1), channel_id=1, source_target_pairs={{4,0},{6,2},{8,4},{10,6},{12,8},{14,10},{16,12},{18,14},{20,16},{2... | collective-permute-start | bytes 983048 | tf_op jit(solution)/shard_map/ppermute | solution.py:17
  63.6 14.0 %copy-start = (f32[96,4,128]{2,1,0:T(4,128)}, f32[96,4,128]{2,1,0:T(4,128)S(1)}, u32[]{:S(2)}) copy-start(f32[96,4,128]{2,1,0:T(4,128)S(1)} %get-tuple-element.366) | copy-start | bytes 589828 | tf_op jit(solution)/shard_map/while
  63.6 14.0 %copy-start.7 = (s32[512]{0:T(512)}, s32[512]{0:T(512)S(1)}, u32[]{:S(2)}) copy-start(s32[512]{0:T(512)S(1)} %get-tuple-element.363) | copy-start | bytes 6148 | tf_op jit(solution)/shard_map/while
  103.9 5.3 %copy-start.6 = (s32[1,1,512]{2,1,0:T(1,128)S(1)}, s32[1,1,512]{2,1,0:T(1,128)}, u32[]{:S(2)}) copy-start(s32[1,1,512]{2,1,0:T(1,128)} %get-tuple-element.403) | copy-start | bytes 6148 | tf_op jit(solution)/shard_map/while
  103.9 5.3 %copy-start.8 = (s32[512]{0:T(512)S(1)}, s32[512]{0:T(512)}, u32[]{:S(2)}) copy-start(s32[512]{0:T(512)} %copy-done.7) | copy-start | bytes 6148 | tf_op jit(solution)/shard_map/while
  109.2 14.0 %copy-start = (f32[96,4,128]{2,1,0:T(4,128)}, f32[96,4,128]{2,1,0:T(4,128)S(1)}, u32[]{:S(2)}) copy-start(f32[96,4,128]{2,1,0:T(4,128)S(1)} %get-tuple-element.366) | copy-start | bytes 589828 | tf_op jit(solution)/shard_map/while
  109.2 14.0 %copy-start.7 = (s32[512]{0:T(512)}, s32[512]{0:T(512)S(1)}, u32[]{:S(2)}) copy-start(s32[512]{0:T(512)S(1)} %get-tuple-element.363) | copy-start | bytes 6148 | tf_op jit(solution)/shard_map/while
  149.5 5.3 %copy-start.8 = (s32[512]{0:T(512)S(1)}, s32[512]{0:T(512)}, u32[]{:S(2)}) copy-start(s32[512]{0:T(512)} %copy-done.7) | copy-start | bytes 6148 | tf_op jit(solution)/shard_map/while
  154.8 14.0 %copy-start = (f32[96,4,128]{2,1,0:T(4,128)}, f32[96,4,128]{2,1,0:T(4,128)S(1)}, u32[]{:S(2)}) copy-start(f32[96,4,128]{2,1,0:T(4,128)S(1)} %get-tuple-element.366) | copy-start | bytes 589828 | tf_op jit(solution)/shard_map/while
  154.8 14.0 %copy-start.7 = (s32[512]{0:T(512)}, s32[512]{0:T(512)S(1)}, u32[]{:S(2)}) copy-start(s32[512]{0:T(512)S(1)} %get-tuple-element.363) | copy-start | bytes 6148 | tf_op jit(solution)/shard_map/while
  195.1 5.3 %copy-start.1 = (f32[96,4,128]{2,1,0:T(4,128)S(1)}, f32[96,4,128]{2,1,0:T(4,128)}, u32[]{:S(2)}) copy-start(f32[96,4,128]{2,1,0:T(4,128)} %copy-done) | copy-start | bytes 589828 | tf_op jit(solution)/shard_map/while
  195.1 5.3 %copy-start.6 = (s32[1,1,512]{2,1,0:T(1,128)S(1)}, s32[1,1,512]{2,1,0:T(1,128)}, u32[]{:S(2)}) copy-start(s32[1,1,512]{2,1,0:T(1,128)} %get-tuple-element.403) | copy-start | bytes 6148 | tf_op jit(solution)/shard_map/while
  195.1 5.3 %copy-start.8 = (s32[512]{0:T(512)S(1)}, s32[512]{0:T(512)}, u32[]{:S(2)}) copy-start(s32[512]{0:T(512)} %copy-done.7) | copy-start | bytes 6148 | tf_op jit(solution)/shard_map/while
  200.4 14.0 %copy-start = (f32[96,4,128]{2,1,0:T(4,128)}, f32[96,4,128]{2,1,0:T(4,128)S(1)}, u32[]{:S(2)}) copy-start(f32[96,4,128]{2,1,0:T(4,128)S(1)} %get-tuple-element.366) | copy-start | bytes 589828 | tf_op jit(solution)/shard_map/while
  200.4 14.0 %copy-start.7 = (s32[512]{0:T(512)}, s32[512]{0:T(512)S(1)}, u32[]{:S(2)}) copy-start(s32[512]{0:T(512)S(1)} %get-tuple-element.363) | copy-start | bytes 6148 | tf_op jit(solution)/shard_map/while
  247.8 6.2 %collective-permute-start.2 = (bf16[16,4096]{1,0:T(8,128)(2,1)S(1)}, bf16[16,4096]{1,0:T(8,128)(2,1)S(1)}, u32[]{:S(2)}, u32[]{:S(2)}) collective-permute-start(bf16[16,4096]{1,0:T(8,128)(2,1)S(1)} %get-tuple-element.239), channel_id=1, source_target_pairs={{0,2},{2,4},{4,6},{6,8},{8,10},{10,12},{12,14},{14,16},{16,18},{18... | collective-permute-start | bytes 393224 | tf_op jit(solution)/shard_map/ppermute | solution.py:17
  249.1 8.0 %collective-permute-start.3 = (bf16[16,4096]{1,0:T(8,128)(2,1)S(1)}, bf16[16,4096]{1,0:T(8,128)(2,1)S(1)}, u32[]{:S(2)}, u32[]{:S(2)}) collective-permute-start(bf16[16,4096]{1,0:T(8,128)(2,1)S(1)} %get-tuple-element.240), channel_id=1, source_target_pairs={{0,4},{2,6},{4,8},{6,10},{8,12},{10,14},{12,16},{14,18},{16,20},{1... | collective-permute-start | bytes 393224 | tf_op jit(solution)/shard_map/ppermute | solution.py:17
  263.9 12.0 %copy-start.3 = (f32[16,4096]{1,0:T(8,128)S(1)}, f32[16,4096]{1,0:T(8,128)}, u32[]{:S(2)}) copy-start(f32[16,4096]{1,0:T(8,128)} %param.13) | copy-start | bytes 786436
  263.9 12.0 %copy-start.4 = (f32[4096]{0:T(1024)S(1)}, f32[4096]{0:T(1024)}, u32[]{:S(2)}) copy-start(f32[4096]{0:T(1024)} %get-tuple-element.207) | copy-start | bytes 49156
  (6 other events, 31.5 us)
Sparse Core Ops, SparseCore 0:
  247.9 13.0 reduce-scatter.1
where the time goes:
time: 285 us; the launch traced here: 284 us
  other arithmetic  142 us (50%)
  local copies, waits for them, and re-layouts  64.7 us (23%)
  matrix products  31.4 us (11%)
  between operations  13.6 us (5%)
  blocking collectives  13.3 us (5%)
  waiting for transfers between devices  8.81 us (3%)
  starting transfers between devices  8.77 us (3%)
    reduce_sum x4, other arithmetic, kernel_tiles(): jnp.sum(offsets * offsets, axis=1) + SOFTENING * SOFTENING  45.9 us
    convert_element_type x4, other arithmetic, kernel_tiles(): (lax.erf(distance * lax.rsqrt(spread)) / distance).astype(jnp.bfloat16)  38.9 us
    scatter-add x4, other arithmetic, pair_step(): row_acc = row_acc.at[left_block].add(forward * alive_now[:, None, None])  20.8 us
    scatter-add x4, other arithmetic, pair_step(): col_acc = col_acc.at[right_block].add(backward * mirror[:, None, None])  20.8 us
    dot_general x4, matrix products, pair_step(): jnp.einsum('pab,pvb->pva', tiles_now, col_vec_blocks[right_block], prefer...  17.8 us
    gather x2, local copies, waits for them, and re-layouts, on_device(): jnp.concatenate([positions, widths[None, :]], axis=0)[:, block_order]  16.3 us
    gather x2, local copies, waits for them, and re-layouts, on_device(): ordered = krylov[:, block_order]  16.3 us
    dot_general x4, matrix products, pair_step(): jnp.einsum('pab,pva->pvb', tiles_now, row_vec_blocks[left_block], preferr...  13.5 us
  transfers between devices with their start and end apart: 5, of which 3 were waited for; matrix products, arithmetic and copies ran while one was open for 0% of the time, Pallas kernels for 0%

commit v1 on v0

v1 whole, which is shorter than its diff:
```python
import functools

import jax
import jax.numpy as jnp
from jax import lax
from jax.experimental import pallas as pl
from jax.experimental.pallas import tpu as pltpu
from jax.sharding import PartitionSpec as P

BLK = 128
SOFTENING = 0.5
UNROLL = 4
CHUNK = 32
VMEM_BYTES = 56 * 1024 * 1024
ERF_POLY = (
    1.1283793236455961,
    0.10276865621773908,
    -0.00019100361666571117,
    -0.0006204428648261939,
    8.78674655970463e-05,
    -5.703654839853857e-06,
    1.4374848121852195e-07,
)


def split3(values):
    high = values.astype(jnp.bfloat16).astype(jnp.float32)
    rest = values - high
    mid = rest.astype(jnp.bfloat16).astype(jnp.float32)
    low = (rest - mid).astype(jnp.bfloat16).astype(jnp.float32)
    return high, mid, low


def gather_kernel(place_ref, type_ref, krylov_ref, order_ref, geometry_ref, vectors_ref, stacked_ref):
    atoms = place_ref.shape[1]
    vecs = krylov_ref.shape[0]
    groups = atoms // BLK
    rows = 16 + vecs
    width = order_ref.shape[1]

    @pl.when(pl.program_id(0) == 0)
    def _():
        high, mid, low = split3(place_ref[...])
        kinds = type_ref[...].astype(jnp.float32)
        empty = jnp.zeros((6, atoms), jnp.float32)
        full = jnp.concatenate([high, mid, low, kinds, empty, krylov_ref[...]], axis=0).astype(jnp.bfloat16)
        for group in range(groups):
            stacked_ref[group * rows : (group + 1) * rows] = full[:, group * BLK : (group + 1) * BLK]

    order = order_ref[...]
    group_of, lane_of = order // BLK, order % BLK
    lane_ids = lax.broadcasted_iota(jnp.int32, (BLK, width), 0)
    picked = (lane_ids == lane_of).astype(jnp.float32).astype(jnp.bfloat16)
    total = jnp.zeros((rows, width), jnp.float32)
    for group in range(groups):
        here = jnp.dot(
            stacked_ref[group * rows : (group + 1) * rows], picked, preferred_element_type=jnp.float32
        )
        total = jnp.where(group_of == group, here, total)
    place = total[0:3] + total[3:6] + total[6:9]
    geometry_ref[...] = jnp.concatenate([place, total[9:10], jnp.zeros((4, width), jnp.float32)], axis=0)
    vectors_ref[...] = total[16:].astype(jnp.bfloat16)


def gathered(positions, atom_type, krylov, order, tile=512):
    vecs, atoms = krylov.shape
    return pl.pallas_call(
        gather_kernel,
        grid=(atoms // tile,),
        in_specs=[
            pl.BlockSpec((3, atoms), lambda step: (0, 0)),
            pl.BlockSpec((1, atoms), lambda step: (0, 0)),
            pl.BlockSpec((vecs, atoms), lambda step: (0, 0)),
            pl.BlockSpec((1, tile), lambda step: (0, step)),
        ],
        out_specs=[
            pl.BlockSpec((8, tile), lambda step: (0, step)),
            pl.BlockSpec((vecs, tile), lambda step: (0, step)),
        ],
        out_shape=[
            jax.ShapeDtypeStruct((8, atoms), jnp.float32),
            jax.ShapeDtypeStruct((vecs, atoms), jnp.bfloat16),
        ],
        scratch_shapes=[pltpu.VMEM((atoms // BLK * (16 + vecs), BLK), jnp.bfloat16)],
        compiler_params=pltpu.CompilerParams(vmem_limit_bytes=VMEM_BYTES),
        cost_estimate=pl.CostEstimate(
            flops=2 * (16 + vecs) * atoms * atoms, bytes_accessed=8 * vecs * atoms, transcendentals=0
        ),
        name="gather_atoms",
    )(positions, atom_type[None, :], krylov, order[None, :])


def scatter_kernel(order_ref, krylov_ref, type_ref, hard_ref, *refs):
    parts, (out_ref, split_ref) = refs[:-2], refs[-2:]
    vecs, atoms = krylov_ref.shape
    groups = atoms // BLK
    chunk = 512
    total = parts[0][...]
    for part in parts[1:]:
        total = total + part[...].astype(jnp.float32)
    high = total.astype(jnp.bfloat16).astype(jnp.float32)
    split_ref[0:vecs] = high
    split_ref[vecs:] = total - high

    lane_ids = lax.broadcasted_iota(jnp.int32, (BLK, chunk), 0)

    def chunk_step(step, total):
        lanes = pl.ds(pl.multiple_of(step * chunk, chunk), chunk)
        order = order_ref[:, lanes]
        group_of, lane_of = order // BLK, order % BLK
        placed = (lane_ids == lane_of).astype(jnp.float32).astype(jnp.bfloat16)
        values = split_ref[:, lanes]
        masked = jnp.concatenate(
            [jnp.where(group_of == group, values, 0.0).astype(jnp.bfloat16) for group in range(groups)], axis=0
        )
        return total + lax.dot_general(
            masked, placed, (((1,), (1,)), ((), ())), preferred_element_type=jnp.float32
        )

    moved = lax.fori_loop(
        0, atoms // chunk, chunk_step, jnp.zeros((groups * 2 * vecs, BLK), jnp.float32)
    )
    kinds = type_ref[...]
    hardness = jnp.zeros((1, atoms), jnp.float32)
    for kind in range(hard_ref.shape[0]):
        hardness = jnp.where(kinds == kind, hard_ref[kind], hardness)
    for group in range(groups):
        lanes = slice(group * BLK, (group + 1) * BLK)
        first = group * 2 * vecs
        placed = moved[first : first + vecs] + moved[first + vecs : first + 2 * vecs]
        out_ref[:, lanes] = placed + hardness[:, lanes] * krylov_ref[:, lanes]


def scattered(order, krylov, atom_type, type_hard, parts):
    vecs, atoms = krylov.shape
    vmem = pl.BlockSpec(memory_space=pltpu.VMEM)
    return pl.pallas_call(
        scatter_kernel,
        in_specs=[vmem] * 3 + [pl.BlockSpec(memory_space=pltpu.SMEM)] + [vmem] * len(parts),
        out_specs=vmem,
        out_shape=jax.ShapeDtypeStruct((vecs, atoms), jnp.float32),
        scratch_shapes=[pltpu.VMEM((2 * vecs, atoms), jnp.float32)],
        compiler_params=pltpu.CompilerParams(vmem_limit_bytes=VMEM_BYTES),
        cost_estimate=pl.CostEstimate(
            flops=4 * vecs * atoms * atoms, bytes_accessed=24 * vecs * atoms, transcendentals=0
        ),
        name="scatter_atoms",
    )(order[None, :], krylov, atom_type[None, :], type_hard, *parts)


def lanes_of(block):
    return pl.ds(pl.multiple_of(block * BLK, BLK), BLK)


def pair_kernel(slabs, left_blocks, left_ids, right_ids, count_ref, table_ref, *refs):
    geo_refs, vec_refs = refs[:slabs], refs[slabs : 2 * slabs]
    out_refs = refs[2 * slabs : 3 * slabs]
    left_ref, origin_ref, geo_ref, mix_ref, vec_ref, acc_ref, both_ref, tile_ref = refs[3 * slabs :]
    atoms = geo_refs[0].shape[1]
    blocks = slabs * atoms // BLK
    row_id = lax.broadcasted_iota(jnp.int32, (8, BLK), 0)
    type_width = table_ref[...]

    for slab in range(slabs):
        geo_ref[:, slab * atoms : (slab + 1) * atoms] = geo_refs[slab][...]
        vec_ref[:, slab * atoms : (slab + 1) * atoms] = vec_refs[slab][...]
    acc_ref[...] = jnp.zeros_like(acc_ref)

    def one_hot(geometry):
        return jnp.where(row_id.astype(jnp.float32) == geometry[3:4, :], 1.0, 0.0)

    def mix_step(block, carry):
        hot = one_hot(geo_ref[:, lanes_of(block)])
        width = jnp.sum(hot * type_width, axis=0, keepdims=True)
        high, mid, low = split3(lax.rsqrt(type_width * type_width + width * width))
        mix_ref[:, lanes_of(block)] = jnp.concatenate([high, mid, low, jnp.zeros_like(low)], axis=0).astype(
            jnp.bfloat16
        )
        return carry

    lax.fori_loop(0, blocks, mix_step, 0)

    def left_step(block, carry):
        geometry = geo_ref[:, lanes_of(block)]
        hot = one_hot(geometry)
        origin = jnp.broadcast_to(geometry[:, 0:1], (8, BLK))
        origin_ref[block] = origin
        local = jnp.where(row_id < 3, geometry - origin, 0.0)
        norm = jnp.sum(local * local, axis=0, keepdims=True) + SOFTENING * SOFTENING
        side = jnp.where(row_id < 3, -2.0 * local, jnp.where(row_id == 3, 1.0, jnp.where(row_id == 4, norm, 0.0)))
        high, mid, low = split3(side)
        rows = jnp.concatenate(
            [high, high, mid, mid, high, low, hot, hot, hot, jnp.zeros((BLK - 72, BLK), jnp.float32)], axis=0
        )
        left_ref[block] = rows.T.astype(jnp.bfloat16)
        return carry

    lax.fori_loop(0, left_blocks, left_step, 0)

    both_ref[...] = jnp.ones_like(both_ref)
    tile_ref[...] = jnp.zeros_like(tile_ref)
    slots = left_ids.shape[0]
    live = count_ref[0]
    zero_side = jnp.zeros((48, BLK), jnp.bfloat16)
    zero_mix = jnp.zeros((32, BLK), jnp.bfloat16)
    zero_tail = jnp.zeros((BLK - 80, 2 * BLK), jnp.bfloat16)

    def weights_of(left, right):
        geometry = geo_ref[:, lanes_of(right)]
        local = jnp.where(row_id < 3, geometry - origin_ref[left], 0.0)
        norm = jnp.sum(local * local, axis=0, keepdims=True)
        side = jnp.where(row_id == 3, norm, jnp.where(row_id == 4, 1.0, local))
        high, mid, low = split3(side)
        rows = jnp.concatenate([high, mid, high, mid, low, high], axis=0).astype(jnp.bfloat16)
        mix = mix_ref[:, lanes_of(right)]
        return jnp.concatenate(
            [
                jnp.concatenate([rows, zero_side], axis=1),
                jnp.concatenate([zero_mix, mix], axis=1),
                zero_tail,
            ],
            axis=0,
        )

    def screened(square, inverse_width):
        inverse = lax.rsqrt(square)
        scaled = square * inverse * inverse_width
        power = scaled * scaled
        series = jnp.float32(ERF_POLY[-1])
        for factor in ERF_POLY[-2::-1]:
            series = series * power + factor
        return (jnp.tanh(scaled * series) * inverse).astype(jnp.bfloat16)

    def slot_ids(turn, offset):
        slot = turn * UNROLL + offset
        place = jnp.clip(slot, 0, slots - 1)
        return left_ids[place], right_ids[place], (slot >= 0) & (slot < live)

    def pair_step(turn, carry):
        done = []
        for offset in range(UNROLL):
            left, right, alive = slot_ids(turn - 2, offset)
            tile = tile_ref[offset]
            forward = lax.dot_general(
                vec_ref[:, lanes_of(right)], tile, (((1,), (1,)), ((), ())), preferred_element_type=jnp.float32
            )
            backward = jnp.dot(vec_ref[:, lanes_of(left)], tile, preferred_element_type=jnp.float32)
            done.append((left, right, forward, backward, alive))
        for offset in range(UNROLL):
            for first in range(0, BLK, CHUNK):
                rows = slice(first, first + CHUNK)
                tile_ref[offset, rows] = screened(both_ref[offset, rows, :BLK], both_ref[offset, rows, BLK:])
        for offset in range(UNROLL):
            left, right, _ = slot_ids(turn, offset)
            both_ref[offset] = jnp.dot(
                left_ref[left], weights_of(left, right), preferred_element_type=jnp.float32
            )
        for left, right, forward, backward, alive in done:
            acc_ref[:, lanes_of(left)] += jnp.where(alive, forward, 0.0)
            acc_ref[:, lanes_of(right)] += jnp.where(alive & (left != right), backward, 0.0)
        return carry

    lax.fori_loop(0, (live + UNROLL - 1) // UNROLL + 2, pair_step, 0)

    for slab in range(slabs):
        out_refs[slab][...] = acc_ref[:, slab * atoms : (slab + 1) * atoms].astype(out_refs[slab].dtype)


def pair_sums(geometries, vectors, left_ids, right_ids, count, table, left_blocks):
    slabs = len(geometries)
    atoms = geometries[0].shape[1]
    vecs = vectors[0].shape[0]
    smem = pl.BlockSpec(memory_space=pltpu.SMEM)
    vmem = pl.BlockSpec(memory_space=pltpu.VMEM)
    kinds = [jnp.float32] + [jnp.bfloat16] * (slabs - 1)
    return pl.pallas_call(
        functools.partial(pair_kernel, slabs, left_blocks),
        in_specs=[smem] * 3 + [vmem] * (1 + 2 * slabs),
        out_specs=[vmem] * slabs,
        out_shape=[jax.ShapeDtypeStruct((vecs, atoms), kind) for kind in kinds],
        scratch_shapes=[
            pltpu.VMEM((left_blocks, BLK, BLK), jnp.bfloat16),
            pltpu.VMEM((left_blocks, 8, BLK), jnp.float32),
            pltpu.VMEM((8, slabs * atoms), jnp.float32),
            pltpu.VMEM((32, slabs * atoms), jnp.bfloat16),
            pltpu.VMEM((vecs, slabs * atoms), jnp.bfloat16),
            pltpu.VMEM((vecs, slabs * atoms), jnp.float32),
            pltpu.VMEM((UNROLL, BLK, 2 * BLK), jnp.float32),
            pltpu.VMEM((UNROLL, BLK, BLK), jnp.bfloat16),
        ],
        compiler_params=pltpu.CompilerParams(vmem_limit_bytes=VMEM_BYTES),
        cost_estimate=pl.CostEstimate(
            flops=left_ids.shape[0] * BLK * BLK * (4 * vecs + 320),
            bytes_accessed=slabs * atoms * (32 + 4 * vecs),
            transcendentals=2 * left_ids.shape[0] * BLK * BLK,
        ),
        name="pair_sums",
    )(left_ids, right_ids, count, table, *geometries, *vectors)


def along_row(value, steps):
    count = lax.axis_size("row")
    first, last = max(0, -steps), min(count, count - steps)
    return lax.ppermute(value, "row", [(source, source + steps) for source in range(first, last)])


def along_col(value, steps):
    count = lax.axis_size("col")
    return lax.ppermute(value, "col", [(source, (source + steps) % count) for source in range(count)])


def on_device(
    positions, atom_type, krylov, block_order, type_width, type_hard, pair_rows, pair_cols, pair_count
):
    vecs, atoms = krylov.shape
    shard_blocks = atoms // BLK
    geometry, vectors = gathered(positions, atom_type, krylov, block_order)

    col_devices = lax.axis_size("col")
    peers = [("col", step) for step in range(1, col_devices)] + [("row", 1), ("row", 2)]
    moved = {"col": along_col, "row": along_row}
    geometries = [geometry] + [moved[axis](geometry, -step) for axis, step in peers]
    panels = [vectors] + [moved[axis](vectors, -step) for axis, step in peers]

    row_index = lax.axis_index("row")
    col_index = lax.axis_index("col")
    rows_list = pair_rows.reshape(-1)
    cols_list = pair_cols.reshape(-1)
    row_slab = (rows_list // shard_blocks - col_index + col_devices) % col_devices
    left_ids = row_slab * shard_blocks + rows_list % shard_blocks
    step = jnp.clip(cols_list // shard_blocks - row_index, 0, 2)
    right_slab = jnp.where(step == 0, 0, step + col_devices - 1)
    right_ids = right_slab * shard_blocks + cols_list % shard_blocks
    table = jnp.zeros((8, BLK), jnp.float32) + jnp.pad(
        type_width, (0, 8 - type_width.shape[0]), constant_values=1.0
    )[:, None]
    sums = pair_sums(
        geometries, panels, left_ids, right_ids, pair_count.reshape(1), table, col_devices * shard_blocks
    )
    returned = [sums[0]] + [moved[axis](part, step) for (axis, step), part in zip(peers, sums[1:])]
    return scattered(block_order, krylov, atom_type, type_hard, returned)


def solution(mesh):
    placed = (
        P(None, ("row", "col")),
        P(("row", "col")),
        P(None, ("row", "col")),
        P(("row", "col")),
        P(),
        P(),
        P("row", "col", None),
        P("row", "col", None),
        P("row", "col"),
    )
    return jax.shard_map(
        on_device, mesh=mesh, in_specs=placed, out_specs=P(None, ("row", "col")), check_vma=False
    )
```

time: 285 us -> 108 us (0.38)
  the two profiles are of different devices: /device:TPU:0 before, /device:TPU:8 now
where the time goes in v1:
time: 108 us
  Pallas kernels  77.5 us (72%)
  starting transfers between devices  15.2 us (14%)
  waiting for transfers between devices  11.8 us (11%)
  local copies, waits for them, and re-layouts  1.8 us (2%)
    pallas_call x1, Pallas kernels, pair_sums(): pl.pallas_call(functools.partial(pair_kernel, slabs, left_blocks), in_spe...  64.2 us
    ppermute x6, starting transfers between devices, along_row(): lax.ppermute(value, 'row', [(source, source + steps) for source in range(...  13.4 us
    pallas_call x1, Pallas kernels, gathered(): pl.pallas_call(gather_kernel, grid=(atoms // tile,), in_specs=[pl.BlockSp...  7.43 us
    ppermute x6, waiting for transfers between devices, along_row(): lax.ppermute(value, 'row', [(source, source + steps) for source in range(...  6.86 us
    pallas_call x1, Pallas kernels, scattered(): pl.pallas_call(scatter_kernel, in_specs=[vmem] * 3 + [pl.BlockSpec(memory...  5.81 us
    ppermute x3, waiting for transfers between devices, along_col(): lax.ppermute(value, 'col', [(source, (source + steps) % count) for source...  4.89 us
  transfers between devices with their start and end apart: 9, of which 5 were waited for; matrix products, arithmetic and copies ran while one was open for 1% of the time, Pallas kernels for 0%

profile of v1, /device:TPU:8, one launch (start us, length us, event | category | flops | bytes accessed | tf_op | source)
XLA Modules:
  0.0 107.6 jit_solution(17946601518137955147)
XLA Ops:
  0.0 7.4 %gather_atoms.1 = (f32[8,4096]{1,0:T(8,128)}, bf16[16,4096]{1,0:T(8,128)(2,1)}) custom-call(f32[3,4096]{1,0:T(4,128)} %place_ref.1, s32[1,4096]{1,0:T(1,128)} %bitcast.10, f32[16,4096]{1,0:T(8,128)} %krylov_ref.3, s32[1,4096]{1,0:T(1,128)} %bitcast.8), custom_call_target="tpu_custom_call" | custom-call | flops 1073741824 | bytes 524288 | tf_op jit(solution)/shard_map/gather_atoms/pallas_call | solution.py:67
  7.4 3.3 %collective-permute-start.2 = (f32[8,4096]{1,0:T(8,128)}, f32[8,4096]{1,0:T(8,128)S(1)}, u32[]{:S(2)}, u32[]{:S(2)}) collective-permute-start(f32[8,4096]{1,0:T(8,128)} %get-tuple-element.11.refs_0_), channel_id=1, source_target_pairs={{4,0},{6,2},{8,4},{10,6},{12,8},{14,10},{16,12},{18,14},{20,16},{2... | collective-permute-start | bytes 393224 | tf_op jit(solution)/shard_map/ppermute | solution.py:304
  10.7 1.9 %collective-permute-start.1 = (f32[8,4096]{1,0:T(8,128)}, f32[8,4096]{1,0:T(8,128)S(1)}, u32[]{:S(2)}, u32[]{:S(2)}) collective-permute-start(f32[8,4096]{1,0:T(8,128)} %get-tuple-element.11.refs_0_), channel_id=1, source_target_pairs={{2,0},{4,2},{6,4},{8,6},{10,8},{12,10},{14,12},{16,14},{18,16},{20... | collective-permute-start | bytes 393224 | tf_op jit(solution)/shard_map/ppermute | solution.py:304
  12.6 1.6 %collective-permute-start = (f32[8,4096]{1,0:T(8,128)}, f32[8,4096]{1,0:T(8,128)S(1)}, u32[]{:S(2)}, u32[]{:S(2)}) collective-permute-start(f32[8,4096]{1,0:T(8,128)} %get-tuple-element.11.refs_0_), channel_id=1, source_target_pairs={{0,1},{1,0},{2,3},{3,2},{4,5},{5,4},{6,7},{7,6},{8,9},{9,8},{10,11... | collective-permute-start | bytes 393224 | tf_op jit(solution)/shard_map/ppermute | solution.py:309
  14.2 2.4 %collective-permute-start.5 = (bf16[16,4096]{1,0:T(8,128)(2,1)}, bf16[16,4096]{1,0:T(8,128)(2,1)S(1)}, u32[]{:S(2)}, u32[]{:S(2)}) collective-permute-start(bf16[16,4096]{1,0:T(8,128)(2,1)} %get-tuple-element.12.refs_4_), channel_id=1, source_target_pairs={{4,0},{6,2},{8,4},{10,6},{12,8},{14,10},{16,12},{18,14},{20,16},{2... | collective-permute-start | bytes 393224 | tf_op jit(solution)/shard_map/ppermute | solution.py:304
  16.7 1.9 %collective-permute-start.4 = (bf16[16,4096]{1,0:T(8,128)(2,1)}, bf16[16,4096]{1,0:T(8,128)(2,1)S(1)}, u32[]{:S(2)}, u32[]{:S(2)}) collective-permute-start(bf16[16,4096]{1,0:T(8,128)(2,1)} %get-tuple-element.12.refs_4_), channel_id=1, source_target_pairs={{2,0},{4,2},{6,4},{8,6},{10,8},{12,10},{14,12},{16,14},{18,16},{20... | collective-permute-start | bytes 393224 | tf_op jit(solution)/shard_map/ppermute | solution.py:304
  18.6 0.0 copy-start.11
  19.3 0.0 copy-start.1
  19.3 0.0 copy-start
  19.3 0.2 collective-permute-start.3
  19.5 0.4 copy-done.1
  20.0 0.0 copy-done
  20.0 0.6 fusion.4
  20.6 1.3 %collective-permute-done.5.refs_7_ = bf16[16,4096]{1,0:T(8,128)(2,1)S(1)} collective-permute-done((bf16[16,4096]{1,0:T(8,128)(2,1)}, bf16[16,4096]{1,0:T(8,128)(2,1)S(1)}, u32[]{:S(2)}, u32[]{:S(2)}) %collective-permute-start.5) | collective-permute-done | bytes 131104 | tf_op jit(solution)/shard_map/ppermute | solution.py:304
  21.9 3.6 %collective-permute-done.3.refs_5_ = bf16[16,4096]{1,0:T(8,128)(2,1)S(1)} collective-permute-done((bf16[16,4096]{1,0:T(8,128)(2,1)}, bf16[16,4096]{1,0:T(8,128)(2,1)S(1)}, u32[]{:S(2)}, u32[]{:S(2)}) %collective-permute-start.3) | collective-permute-done | bytes 131104 | tf_op jit(solution)/shard_map/ppermute | solution.py:309
  25.5 0.7 add.42.table_ref
  26.2 64.2 %pair_sums.1 = (f32[16,4096]{1,0:T(8,128)}, bf16[16,4096]{1,0:T(8,128)(2,1)}, bf16[16,4096]{1,0:T(8,128)(2,1)}, bf16[16,4096]{1,0:T(8,128)(2,1)}) custom-call(s32[512]{0:T(512)} %get-tuple-element.17.left_ids, s32[512]{0:T(512)} %get-tuple-element.18.right_ids, s32[1]{0:T(128)} %bitcast.5.count_ref, f32[8,128]{1,0:T(8,128)} %add.42.table_ref, ...), custom_call_target="tpu_custom_call" | custom-call | flops 3221225472 | bytes 1572864 | tf_op jit(solution)/shard_map/pair_sums/pallas_call | solution.py:276
  90.4 1.9 %collective-permute-start.7 = (bf16[16,4096]{1,0:T(8,128)(2,1)}, bf16[16,4096]{1,0:T(8,128)(2,1)S(1)}, u32[]{:S(2)}, u32[]{:S(2)}) collective-permute-start(bf16[16,4096]{1,0:T(8,128)(2,1)} %get-tuple-element.15), channel_id=1, source_target_pairs={{0,2},{2,4},{4,6},{6,8},{8,10},{10,12},{12,14},{14,16},{16,18},{18... | collective-permute-start | bytes 393224 | tf_op jit(solution)/shard_map/ppermute | solution.py:304
  92.4 1.9 %collective-permute-start.8 = (bf16[16,4096]{1,0:T(8,128)(2,1)}, bf16[16,4096]{1,0:T(8,128)(2,1)S(1)}, u32[]{:S(2)}, u32[]{:S(2)}) collective-permute-start(bf16[16,4096]{1,0:T(8,128)(2,1)} %get-tuple-element.16), channel_id=1, source_target_pairs={{0,4},{2,6},{4,8},{6,10},{8,12},{10,14},{12,16},{14,18},{16,20},{1... | collective-permute-start | bytes 393224 | tf_op jit(solution)/shard_map/ppermute | solution.py:304
  94.3 1.3 %collective-permute-done.6.refs_1_ = bf16[16,4096]{1,0:T(8,128)(2,1)S(1)} collective-permute-done((bf16[16,4096]{1,0:T(8,128)(2,1)}, bf16[16,4096]{1,0:T(8,128)(2,1)S(1)}, u32[]{:S(2)}, u32[]{:S(2)}) %collective-permute-start.6) | collective-permute-done | bytes 131104 | tf_op jit(solution)/shard_map/ppermute | solution.py:309
  95.6 2.2 %collective-permute-done.7.refs_2_ = bf16[16,4096]{1,0:T(8,128)(2,1)S(1)} collective-permute-done((bf16[16,4096]{1,0:T(8,128)(2,1)}, bf16[16,4096]{1,0:T(8,128)(2,1)S(1)}, u32[]{:S(2)}, u32[]{:S(2)}) %collective-permute-start.7) | collective-permute-done | bytes 131104 | tf_op jit(solution)/shard_map/ppermute | solution.py:304
  97.8 3.3 %collective-permute-done.8.refs_3_ = bf16[16,4096]{1,0:T(8,128)(2,1)S(1)} collective-permute-done((bf16[16,4096]{1,0:T(8,128)(2,1)}, bf16[16,4096]{1,0:T(8,128)(2,1)S(1)}, u32[]{:S(2)}, u32[]{:S(2)}) %collective-permute-start.8) | collective-permute-done | bytes 131104 | tf_op jit(solution)/shard_map/ppermute | solution.py:304
  101.2 0.6 copy-done.10
  101.8 5.8 %scatter_atoms.1 = f32[16,4096]{1,0:T(8,128)} custom-call(s32[1,4096]{1,0:T(1,128)} %bitcast.9, f32[16,4096]{1,0:T(8,128)} %krylov_ref.3, s32[1,4096]{1,0:T(1,128)} %bitcast.11, f32[6]{0:T(128)} %hard_ref.1, f32[16,4096]{1,0:T(8,128)} %get-tuple-element.13.refs_0_, bf16[16,4096]{1,0:T(8,128)(2,1)} %copy-done.8, bf16[16,4096]{1,0:T(8,128)(2,1)} %copy-done.9, ...), custom_call_target="tpu_custom_call" | custom-call | flops 1073741824 | bytes 1572864 | tf_op jit(solution)/shard_map/scatter_atoms/pallas_call | solution.py:137
  (24 shorter events, 0.1 us)
Async XLA Ops:
  7.4 11.9 %collective-permute-start.2 = (f32[8,4096]{1,0:T(8,128)}, f32[8,4096]{1,0:T(8,128)S(1)}, u32[]{:S(2)}, u32[]{:S(2)}) collective-permute-start(f32[8,4096]{1,0:T(8,128)} %get-tuple-element.11.refs_0_), channel_id=1, source_target_pairs={{4,0},{6,2},{8,4},{10,6},{12,8},{14,10},{16,12},{18,14},{20,16},{2... | collective-permute-start | bytes 393224 | tf_op jit(solution)/shard_map/ppermute | solution.py:304
  10.7 9.9 %collective-permute-start.1 = (f32[8,4096]{1,0:T(8,128)}, f32[8,4096]{1,0:T(8,128)S(1)}, u32[]{:S(2)}, u32[]{:S(2)}) collective-permute-start(f32[8,4096]{1,0:T(8,128)} %get-tuple-element.11.refs_0_), channel_id=1, source_target_pairs={{2,0},{4,2},{6,4},{8,6},{10,8},{12,10},{14,12},{16,14},{18,16},{20... | collective-permute-start | bytes 393224 | tf_op jit(solution)/shard_map/ppermute | solution.py:304
  12.6 8.0 %collective-permute-start = (f32[8,4096]{1,0:T(8,128)}, f32[8,4096]{1,0:T(8,128)S(1)}, u32[]{:S(2)}, u32[]{:S(2)}) collective-permute-start(f32[8,4096]{1,0:T(8,128)} %get-tuple-element.11.refs_0_), channel_id=1, source_target_pairs={{0,1},{1,0},{2,3},{3,2},{4,5},{5,4},{6,7},{7,6},{8,9},{9,8},{10,11... | collective-permute-start | bytes 393224 | tf_op jit(solution)/shard_map/ppermute | solution.py:309
  14.2 7.7 %collective-permute-start.5 = (bf16[16,4096]{1,0:T(8,128)(2,1)}, bf16[16,4096]{1,0:T(8,128)(2,1)S(1)}, u32[]{:S(2)}, u32[]{:S(2)}) collective-permute-start(bf16[16,4096]{1,0:T(8,128)(2,1)} %get-tuple-element.12.refs_4_), channel_id=1, source_target_pairs={{4,0},{6,2},{8,4},{10,6},{12,8},{14,10},{16,12},{18,14},{20,16},{2... | collective-permute-start | bytes 393224 | tf_op jit(solution)/shard_map/ppermute | solution.py:304
  16.7 5.3 %collective-permute-start.4 = (bf16[16,4096]{1,0:T(8,128)(2,1)}, bf16[16,4096]{1,0:T(8,128)(2,1)S(1)}, u32[]{:S(2)}, u32[]{:S(2)}) collective-permute-start(bf16[16,4096]{1,0:T(8,128)(2,1)} %get-tuple-element.12.refs_4_), channel_id=1, source_target_pairs={{2,0},{4,2},{6,4},{8,6},{10,8},{12,10},{14,12},{16,14},{18,16},{20... | collective-permute-start | bytes 393224 | tf_op jit(solution)/shard_map/ppermute | solution.py:304
  18.6 0.7 copy-start.11
  19.3 0.7 copy-start.1
  19.3 0.7 copy-start
  19.3 6.9 %copy-start.2 = (f32[8,4096]{1,0:T(8,128)}, f32[8,4096]{1,0:T(8,128)S(1)}, u32[]{:S(2)}) copy-start(f32[8,4096]{1,0:T(8,128)S(1)} %collective-permute-done.2.refs_3_) | copy-start | bytes 393220
  19.3 6.2 %collective-permute-start.3 = (bf16[16,4096]{1,0:T(8,128)(2,1)}, bf16[16,4096]{1,0:T(8,128)(2,1)S(1)}, u32[]{:S(2)}, u32[]{:S(2)}) collective-permute-start(bf16[16,4096]{1,0:T(8,128)(2,1)} %get-tuple-element.12.refs_4_), channel_id=1, source_target_pairs={{0,1},{1,0},{2,3},{3,2},{4,5},{5,4},{6,7},{7,6},{8,9},{9,8},{10,11... | collective-permute-start | bytes 393224 | tf_op jit(solution)/shard_map/ppermute | solution.py:309
  20.6 5.6 %copy-start.3 = (f32[8,4096]{1,0:T(8,128)}, f32[8,4096]{1,0:T(8,128)S(1)}, u32[]{:S(2)}) copy-start(f32[8,4096]{1,0:T(8,128)S(1)} %collective-permute-done.1.refs_2_) | copy-start | bytes 393220
  20.6 5.6 %copy-start.4 = (f32[8,4096]{1,0:T(8,128)}, f32[8,4096]{1,0:T(8,128)S(1)}, u32[]{:S(2)}) copy-start(f32[8,4096]{1,0:T(8,128)S(1)} %collective-permute-done.refs_1_) | copy-start | bytes 393220
  21.9 4.2 %copy-start.5 = (bf16[16,4096]{1,0:T(8,128)(2,1)}, bf16[16,4096]{1,0:T(8,128)(2,1)S(1)}, u32[]{:S(2)}) copy-start(bf16[16,4096]{1,0:T(8,128)(2,1)S(1)} %collective-permute-done.5.refs_7_) | copy-start | bytes 393220
  21.9 4.2 %copy-start.6 = (bf16[16,4096]{1,0:T(8,128)(2,1)}, bf16[16,4096]{1,0:T(8,128)(2,1)S(1)}, u32[]{:S(2)}) copy-start(bf16[16,4096]{1,0:T(8,128)(2,1)S(1)} %collective-permute-done.4.refs_6_) | copy-start | bytes 393220
  25.5 0.7 copy-start.7
  90.4 5.2 %collective-permute-start.6 = (bf16[16,4096]{1,0:T(8,128)(2,1)}, bf16[16,4096]{1,0:T(8,128)(2,1)S(1)}, u32[]{:S(2)}, u32[]{:S(2)}) collective-permute-start(bf16[16,4096]{1,0:T(8,128)(2,1)} %get-tuple-element.14), channel_id=1, source_target_pairs={{0,1},{1,0},{2,3},{3,2},{4,5},{5,4},{6,7},{7,6},{8,9},{9,8},{10,11... | collective-permute-start | bytes 393224 | tf_op jit(solution)/shard_map/ppermute | solution.py:309
  90.4 7.4 %collective-permute-start.7 = (bf16[16,4096]{1,0:T(8,128)(2,1)}, bf16[16,4096]{1,0:T(8,128)(2,1)S(1)}, u32[]{:S(2)}, u32[]{:S(2)}) collective-permute-start(bf16[16,4096]{1,0:T(8,128)(2,1)} %get-tuple-element.15), channel_id=1, source_target_pairs={{0,2},{2,4},{4,6},{6,8},{8,10},{10,12},{12,14},{14,16},{16,18},{18... | collective-permute-start | bytes 393224 | tf_op jit(solution)/shard_map/ppermute | solution.py:304
  92.4 8.8 %collective-permute-start.8 = (bf16[16,4096]{1,0:T(8,128)(2,1)}, bf16[16,4096]{1,0:T(8,128)(2,1)S(1)}, u32[]{:S(2)}, u32[]{:S(2)}) collective-permute-start(bf16[16,4096]{1,0:T(8,128)(2,1)} %get-tuple-element.16), channel_id=1, source_target_pairs={{0,4},{2,6},{4,8},{6,10},{8,12},{10,14},{12,16},{14,18},{16,20},{1... | collective-permute-start | bytes 393224 | tf_op jit(solution)/shard_map/ppermute | solution.py:304
  95.6 5.6 %copy-start.8 = (bf16[16,4096]{1,0:T(8,128)(2,1)}, bf16[16,4096]{1,0:T(8,128)(2,1)S(1)}, u32[]{:S(2)}) copy-start(bf16[16,4096]{1,0:T(8,128)(2,1)S(1)} %collective-permute-done.6.refs_1_) | copy-start | bytes 393220
  97.8 3.3 %copy-start.9 = (bf16[16,4096]{1,0:T(8,128)(2,1)}, bf16[16,4096]{1,0:T(8,128)(2,1)S(1)}, u32[]{:S(2)}) copy-start(bf16[16,4096]{1,0:T(8,128)(2,1)S(1)} %collective-permute-done.7.refs_2_) | copy-start | bytes 393220
  101.2 0.6 copy-start.10

commit v2 on v1

--- a/solution.py
+++ b/solution.py
@@ -12,14 +12,12 @@
 UNROLL = 4
 CHUNK = 32
 VMEM_BYTES = 56 * 1024 * 1024
-ERF_POLY = (
-    1.1283793236455961,
-    0.10276865621773908,
-    -0.00019100361666571117,
-    -0.0006204428648261939,
-    8.78674655970463e-05,
-    -5.703654839853857e-06,
-    1.4374848121852195e-07,
+SLOPE = 1.1283737853323306
+ERF_SERIES = (
+    0.07159415430567773,
+    -0.00022649025157034893,
+    -0.000190667906232071,
+    1.1875337467865749e-05,
 )
 
 
@@ -172,13 +170,13 @@
     def mix_step(block, carry):
         hot = one_hot(geo_ref[:, lanes_of(block)])
         width = jnp.sum(hot * type_width, axis=0, keepdims=True)
-        high, mid, low = split3(lax.rsqrt(type_width * type_width + width * width))
+        high, mid, low = split3(SLOPE * lax.rsqrt(type_width * type_width + width * width))
         mix_ref[:, lanes_of(block)] = jnp.concatenate([high, mid, low, jnp.zeros_like(low)], axis=0).astype(
             jnp.bfloat16
         )
         return carry
 
-    lax.fori_loop(0, blocks, mix_step, 0)
+    lax.fori_loop(0, blocks, mix_step, 0, unroll=4)
 
     def left_step(block, carry):
         geometry = geo_ref[:, lanes_of(block)]
@@ -195,7 +193,7 @@
         left_ref[block] = rows.T.astype(jnp.bfloat16)
         return carry
 
-    lax.fori_loop(0, left_blocks, left_step, 0)
+    lax.fori_loop(0, left_blocks, left_step, 0, unroll=4)
 
     both_ref[...] = jnp.ones_like(both_ref)
     tile_ref[...] = jnp.zeros_like(tile_ref)
@@ -225,11 +223,12 @@
     def screened(square, inverse_width):
         inverse = lax.rsqrt(square)
         scaled = square * inverse * inverse_width
-        power = scaled * scaled
-        series = jnp.float32(ERF_POLY[-1])
-        for factor in ERF_POLY[-2::-1]:
-            series = series * power + factor
-        return (jnp.tanh(scaled * series) * inverse).astype(jnp.bfloat16)
+        narrow = scaled.astype(jnp.bfloat16)
+        power = narrow * narrow
+        series = jnp.bfloat16(ERF_SERIES[-1])
+        for factor in ERF_SERIES[-2::-1] + (1.0,):
+            series = series * power + jnp.bfloat16(factor)
+        return (jnp.tanh(narrow * series).astype(jnp.float32) * inverse).astype(jnp.bfloat16)
 
     def slot_ids(turn, offset):
         slot = turn * UNROLL + offset

time: 108 us -> 90.3 us (0.84)
  the two profiles are of different devices: /device:TPU:8 before, /device:TPU:16 now
where the time goes in v2:
time: 90.3 us; the launch traced here: 89.1 us
  Pallas kernels  48.8 us (54%)
  starting transfers between devices  28.7 us (32%)
  waiting for transfers between devices  8.84 us (10%)
  local copies, waits for them, and re-layouts  1.42 us (2%)
    pallas_call x1, Pallas kernels, pair_sums(): pl.pallas_call(functools.partial(pair_kernel, slabs, left_blocks), in_spe...  35.5 us
    ppermute x6, starting transfers between devices, along_row(): lax.ppermute(value, 'row', [(source, source + steps) for source in range(...  23.3 us
    pallas_call x1, Pallas kernels, gathered(): pl.pallas_call(gather_kernel, grid=(atoms // tile,), in_specs=[pl.BlockSp...  7.43 us
    pallas_call x1, Pallas kernels, scattered(): pl.pallas_call(scatter_kernel, in_specs=[vmem] * 3 + [pl.BlockSpec(memory...  5.81 us
    ppermute x3, starting transfers between devices, along_col(): lax.ppermute(value, 'col', [(source, (source + steps) % count) for source...  5.43 us
    ppermute x6, waiting for transfers between devices, along_row(): lax.ppermute(value, 'row', [(source, source + steps) for source in range(...  5.12 us
    ppermute x3, waiting for transfers between devices, along_col(): lax.ppermute(value, 'col', [(source, (source + steps) % count) for source...  3.72 us
  transfers between devices with their start and end apart: 9, of which 4 were waited for; matrix products, arithmetic and copies ran while one was open for 1% of the time, Pallas kernels for 0%

profile of v2, /device:TPU:16, one launch (start us, length us, event | category | flops | bytes accessed | tf_op | source)
XLA Modules:
  0.0 89.1 jit_solution(14231288145697947135)
XLA Ops:
  0.0 7.4 %gather_atoms.1 = (f32[8,4096]{1,0:T(8,128)}, bf16[16,4096]{1,0:T(8,128)(2,1)}) custom-call(f32[3,4096]{1,0:T(4,128)} %place_ref.1, s32[1,4096]{1,0:T(1,128)} %bitcast.10, f32[16,4096]{1,0:T(8,128)} %krylov_ref.3, s32[1,4096]{1,0:T(1,128)} %bitcast.8), custom_call_target="tpu_custom_call" | custom-call | flops 1073741824 | bytes 524288 | tf_op jit(solution)/shard_map/gather_atoms/pallas_call | solution.py:65
  7.4 3.3 %collective-permute-start.2 = (f32[8,4096]{1,0:T(8,128)}, f32[8,4096]{1,0:T(8,128)S(1)}, u32[]{:S(2)}, u32[]{:S(2)}) collective-permute-start(f32[8,4096]{1,0:T(8,128)} %get-tuple-element.11.refs_0_), channel_id=1, source_target_pairs={{4,0},{6,2},{8,4},{10,6},{12,8},{14,10},{16,12},{18,14},{20,16},{2... | collective-permute-start | bytes 393224 | tf_op jit(solution)/shard_map/ppermute | solution.py:303
  10.7 1.9 %collective-permute-start.1 = (f32[8,4096]{1,0:T(8,128)}, f32[8,4096]{1,0:T(8,128)S(1)}, u32[]{:S(2)}, u32[]{:S(2)}) collective-permute-start(f32[8,4096]{1,0:T(8,128)} %get-tuple-element.11.refs_0_), channel_id=1, source_target_pairs={{2,0},{4,2},{6,4},{8,6},{10,8},{12,10},{14,12},{16,14},{18,16},{20... | collective-permute-start | bytes 393224 | tf_op jit(solution)/shard_map/ppermute | solution.py:303
  12.6 1.6 %collective-permute-start = (f32[8,4096]{1,0:T(8,128)}, f32[8,4096]{1,0:T(8,128)S(1)}, u32[]{:S(2)}, u32[]{:S(2)}) collective-permute-start(f32[8,4096]{1,0:T(8,128)} %get-tuple-element.11.refs_0_), channel_id=1, source_target_pairs={{0,1},{1,0},{2,3},{3,2},{4,5},{5,4},{6,7},{7,6},{8,9},{9,8},{10,11... | collective-permute-start | bytes 393224 | tf_op jit(solution)/shard_map/ppermute | solution.py:308
  14.2 3.0 %collective-permute-start.5 = (bf16[16,4096]{1,0:T(8,128)(2,1)}, bf16[16,4096]{1,0:T(8,128)(2,1)S(1)}, u32[]{:S(2)}, u32[]{:S(2)}) collective-permute-start(bf16[16,4096]{1,0:T(8,128)(2,1)} %get-tuple-element.12.refs_4_), channel_id=1, source_target_pairs={{4,0},{6,2},{8,4},{10,6},{12,8},{14,10},{16,12},{18,14},{20,16},{2... | collective-permute-start | bytes 393224 | tf_op jit(solution)/shard_map/ppermute | solution.py:303
  17.2 2.3 %collective-permute-start.4 = (bf16[16,4096]{1,0:T(8,128)(2,1)}, bf16[16,4096]{1,0:T(8,128)(2,1)S(1)}, u32[]{:S(2)}, u32[]{:S(2)}) collective-permute-start(bf16[16,4096]{1,0:T(8,128)(2,1)} %get-tuple-element.12.refs_4_), channel_id=1, source_target_pairs={{2,0},{4,2},{6,4},{8,6},{10,8},{12,10},{14,12},{16,14},{18,16},{20... | collective-permute-start | bytes 393224 | tf_op jit(solution)/shard_map/ppermute | solution.py:303
  19.5 0.0 copy-start.11
  20.2 0.0 copy-start.1
  20.2 0.0 copy-start
  20.2 0.6 collective-permute-start.3
  20.8 0.1 copy-done.1
  20.9 0.0 copy-done
  20.9 0.6 fusion.4
  21.5 0.4 collective-permute-done.5.refs_7_
  21.9 0.4 collective-permute-done.4.refs_6_
  22.3 3.7 %collective-permute-done.3.refs_5_ = bf16[16,4096]{1,0:T(8,128)(2,1)S(1)} collective-permute-done((bf16[16,4096]{1,0:T(8,128)(2,1)}, bf16[16,4096]{1,0:T(8,128)(2,1)S(1)}, u32[]{:S(2)}, u32[]{:S(2)}) %collective-permute-start.3) | collective-permute-done | bytes 131104 | tf_op jit(solution)/shard_map/ppermute | solution.py:308
  26.0 0.7 add.42.table_ref
  26.7 35.5 %pair_sums.1 = (f32[16,4096]{1,0:T(8,128)}, bf16[16,4096]{1,0:T(8,128)(2,1)}, bf16[16,4096]{1,0:T(8,128)(2,1)}, bf16[16,4096]{1,0:T(8,128)(2,1)}) custom-call(s32[512]{0:T(512)} %get-tuple-element.17.left_ids, s32[512]{0:T(512)} %get-tuple-element.18.right_ids, s32[1]{0:T(128)} %bitcast.5.count_ref, f32[8,128]{1,0:T(8,128)} %add.42.table_ref, ...), custom_call_target="tpu_custom_call" | custom-call | flops 3221225472 | bytes 1572864 | tf_op jit(solution)/shard_map/pair_sums/pallas_call | solution.py:275
  62.2 3.3 %collective-permute-start.6 = (bf16[16,4096]{1,0:T(8,128)(2,1)}, bf16[16,4096]{1,0:T(8,128)(2,1)S(1)}, u32[]{:S(2)}, u32[]{:S(2)}) collective-permute-start(bf16[16,4096]{1,0:T(8,128)(2,1)} %get-tuple-element.14), channel_id=1, source_target_pairs={{0,1},{1,0},{2,3},{3,2},{4,5},{5,4},{6,7},{7,6},{8,9},{9,8},{10,11... | collective-permute-start | bytes 393224 | tf_op jit(solution)/shard_map/ppermute | solution.py:308
  65.5 8.8 %collective-permute-start.7 = (bf16[16,4096]{1,0:T(8,128)(2,1)}, bf16[16,4096]{1,0:T(8,128)(2,1)S(1)}, u32[]{:S(2)}, u32[]{:S(2)}) collective-permute-start(bf16[16,4096]{1,0:T(8,128)(2,1)} %get-tuple-element.15), channel_id=1, source_target_pairs={{0,2},{2,4},{4,6},{6,8},{8,10},{10,12},{12,14},{14,16},{16,18},{18... | collective-permute-start | bytes 393224 | tf_op jit(solution)/shard_map/ppermute | solution.py:303
  74.3 4.0 %collective-permute-start.8 = (bf16[16,4096]{1,0:T(8,128)(2,1)}, bf16[16,4096]{1,0:T(8,128)(2,1)S(1)}, u32[]{:S(2)}, u32[]{:S(2)}) collective-permute-start(bf16[16,4096]{1,0:T(8,128)(2,1)} %get-tuple-element.16), channel_id=1, source_target_pairs={{0,4},{2,6},{4,8},{6,10},{8,12},{10,14},{12,16},{14,18},{16,20},{1... | collective-permute-start | bytes 393224 | tf_op jit(solution)/shard_map/ppermute | solution.py:303
  78.4 4.3 %collective-permute-done.8.refs_3_ = bf16[16,4096]{1,0:T(8,128)(2,1)S(1)} collective-permute-done((bf16[16,4096]{1,0:T(8,128)(2,1)}, bf16[16,4096]{1,0:T(8,128)(2,1)S(1)}, u32[]{:S(2)}, u32[]{:S(2)}) %collective-permute-start.8) | collective-permute-done | bytes 131104 | tf_op jit(solution)/shard_map/ppermute | solution.py:303
  82.7 0.6 copy-done.10
  83.3 5.8 %scatter_atoms.1 = f32[16,4096]{1,0:T(8,128)} custom-call(s32[1,4096]{1,0:T(1,128)} %bitcast.9, f32[16,4096]{1,0:T(8,128)} %krylov_ref.3, s32[1,4096]{1,0:T(1,128)} %bitcast.11, f32[6]{0:T(128)} %hard_ref.1, f32[16,4096]{1,0:T(8,128)} %get-tuple-element.13.refs_0_, bf16[16,4096]{1,0:T(8,128)(2,1)} %copy-done.8, bf16[16,4096]{1,0:T(8,128)(2,1)} %copy-done.9, ...), custom_call_target="tpu_custom_call" | custom-call | flops 1073741824 | bytes 1572864 | tf_op jit(solution)/shard_map/scatter_atoms/pallas_call | solution.py:135
  (24 shorter events, 0.1 us)
Async XLA Ops:
  7.4 12.8 %collective-permute-start.2 = (f32[8,4096]{1,0:T(8,128)}, f32[8,4096]{1,0:T(8,128)S(1)}, u32[]{:S(2)}, u32[]{:S(2)}) collective-permute-start(f32[8,4096]{1,0:T(8,128)} %get-tuple-element.11.refs_0_), channel_id=1, source_target_pairs={{4,0},{6,2},{8,4},{10,6},{12,8},{14,10},{16,12},{18,14},{20,16},{2... | collective-permute-start | bytes 393224 | tf_op jit(solution)/shard_map/ppermute | solution.py:303
  10.7 10.8 %collective-permute-start.1 = (f32[8,4096]{1,0:T(8,128)}, f32[8,4096]{1,0:T(8,128)S(1)}, u32[]{:S(2)}, u32[]{:S(2)}) collective-permute-start(f32[8,4096]{1,0:T(8,128)} %get-tuple-element.11.refs_0_), channel_id=1, source_target_pairs={{2,0},{4,2},{6,4},{8,6},{10,8},{12,10},{14,12},{16,14},{18,16},{20... | collective-permute-start | bytes 393224 | tf_op jit(solution)/shard_map/ppermute | solution.py:303
  12.6 8.9 %collective-permute-start = (f32[8,4096]{1,0:T(8,128)}, f32[8,4096]{1,0:T(8,128)S(1)}, u32[]{:S(2)}, u32[]{:S(2)}) collective-permute-start(f32[8,4096]{1,0:T(8,128)} %get-tuple-element.11.refs_0_), channel_id=1, source_target_pairs={{0,1},{1,0},{2,3},{3,2},{4,5},{5,4},{6,7},{7,6},{8,9},{9,8},{10,11... | collective-permute-start | bytes 393224 | tf_op jit(solution)/shard_map/ppermute | solution.py:308
  14.2 7.7 %collective-permute-start.5 = (bf16[16,4096]{1,0:T(8,128)(2,1)}, bf16[16,4096]{1,0:T(8,128)(2,1)S(1)}, u32[]{:S(2)}, u32[]{:S(2)}) collective-permute-start(bf16[16,4096]{1,0:T(8,128)(2,1)} %get-tuple-element.12.refs_4_), channel_id=1, source_target_pairs={{4,0},{6,2},{8,4},{10,6},{12,8},{14,10},{16,12},{18,14},{20,16},{2... | collective-permute-start | bytes 393224 | tf_op jit(solution)/shard_map/ppermute | solution.py:303
  17.2 5.1 %collective-permute-start.4 = (bf16[16,4096]{1,0:T(8,128)(2,1)}, bf16[16,4096]{1,0:T(8,128)(2,1)S(1)}, u32[]{:S(2)}, u32[]{:S(2)}) collective-permute-start(bf16[16,4096]{1,0:T(8,128)(2,1)} %get-tuple-element.12.refs_4_), channel_id=1, source_target_pairs={{2,0},{4,2},{6,4},{8,6},{10,8},{12,10},{14,12},{16,14},{18,16},{20... | collective-permute-start | bytes 393224 | tf_op jit(solution)/shard_map/ppermute | solution.py:303
  19.5 0.7 copy-start.11
  20.2 0.7 copy-start.1
  20.2 0.7 copy-start
  20.2 6.5 %copy-start.2 = (f32[8,4096]{1,0:T(8,128)}, f32[8,4096]{1,0:T(8,128)S(1)}, u32[]{:S(2)}) copy-start(f32[8,4096]{1,0:T(8,128)S(1)} %collective-permute-done.2.refs_3_) | copy-start | bytes 393220
  20.2 5.8 %collective-permute-start.3 = (bf16[16,4096]{1,0:T(8,128)(2,1)}, bf16[16,4096]{1,0:T(8,128)(2,1)S(1)}, u32[]{:S(2)}, u32[]{:S(2)}) collective-permute-start(bf16[16,4096]{1,0:T(8,128)(2,1)} %get-tuple-element.12.refs_4_), channel_id=1, source_target_pairs={{0,1},{1,0},{2,3},{3,2},{4,5},{5,4},{6,7},{7,6},{8,9},{9,8},{10,11... | collective-permute-start | bytes 393224 | tf_op jit(solution)/shard_map/ppermute | solution.py:308
  21.5 5.2 %copy-start.3 = (f32[8,4096]{1,0:T(8,128)}, f32[8,4096]{1,0:T(8,128)S(1)}, u32[]{:S(2)}) copy-start(f32[8,4096]{1,0:T(8,128)S(1)} %collective-permute-done.1.refs_2_) | copy-start | bytes 393220
  21.5 5.2 %copy-start.4 = (f32[8,4096]{1,0:T(8,128)}, f32[8,4096]{1,0:T(8,128)S(1)}, u32[]{:S(2)}) copy-start(f32[8,4096]{1,0:T(8,128)S(1)} %collective-permute-done.refs_1_) | copy-start | bytes 393220
  21.9 4.8 %copy-start.5 = (bf16[16,4096]{1,0:T(8,128)(2,1)}, bf16[16,4096]{1,0:T(8,128)(2,1)S(1)}, u32[]{:S(2)}) copy-start(bf16[16,4096]{1,0:T(8,128)(2,1)S(1)} %collective-permute-done.5.refs_7_) | copy-start | bytes 393220
  22.3 4.4 %copy-start.6 = (bf16[16,4096]{1,0:T(8,128)(2,1)}, bf16[16,4096]{1,0:T(8,128)(2,1)S(1)}, u32[]{:S(2)}) copy-start(bf16[16,4096]{1,0:T(8,128)(2,1)S(1)} %collective-permute-done.4.refs_6_) | copy-start | bytes 393220
  26.0 0.7 copy-start.7
  62.2 16.1 %collective-permute-start.6 = (bf16[16,4096]{1,0:T(8,128)(2,1)}, bf16[16,4096]{1,0:T(8,128)(2,1)S(1)}, u32[]{:S(2)}, u32[]{:S(2)}) collective-permute-start(bf16[16,4096]{1,0:T(8,128)(2,1)} %get-tuple-element.14), channel_id=1, source_target_pairs={{0,1},{1,0},{2,3},{3,2},{4,5},{5,4},{6,7},{7,6},{8,9},{9,8},{10,11... | collective-permute-start | bytes 393224 | tf_op jit(solution)/shard_map/ppermute | solution.py:308
  65.5 12.8 %collective-permute-start.7 = (bf16[16,4096]{1,0:T(8,128)(2,1)}, bf16[16,4096]{1,0:T(8,128)(2,1)S(1)}, u32[]{:S(2)}, u32[]{:S(2)}) collective-permute-start(bf16[16,4096]{1,0:T(8,128)(2,1)} %get-tuple-element.15), channel_id=1, source_target_pairs={{0,2},{2,4},{4,6},{6,8},{8,10},{10,12},{12,14},{14,16},{16,18},{18... | collective-permute-start | bytes 393224 | tf_op jit(solution)/shard_map/ppermute | solution.py:303
  74.3 8.4 %collective-permute-start.8 = (bf16[16,4096]{1,0:T(8,128)(2,1)}, bf16[16,4096]{1,0:T(8,128)(2,1)S(1)}, u32[]{:S(2)}, u32[]{:S(2)}) collective-permute-start(bf16[16,4096]{1,0:T(8,128)(2,1)} %get-tuple-element.16), channel_id=1, source_target_pairs={{0,4},{2,6},{4,8},{6,10},{8,12},{10,14},{12,16},{14,18},{16,20},{1... | collective-permute-start | bytes 393224 | tf_op jit(solution)/shard_map/ppermute | solution.py:303
  78.3 4.4 %copy-start.8 = (bf16[16,4096]{1,0:T(8,128)(2,1)}, bf16[16,4096]{1,0:T(8,128)(2,1)S(1)}, u32[]{:S(2)}) copy-start(bf16[16,4096]{1,0:T(8,128)(2,1)S(1)} %collective-permute-done.6.refs_1_) | copy-start | bytes 393220
  78.4 4.3 %copy-start.9 = (bf16[16,4096]{1,0:T(8,128)(2,1)}, bf16[16,4096]{1,0:T(8,128)(2,1)S(1)}, u32[]{:S(2)}) copy-start(bf16[16,4096]{1,0:T(8,128)(2,1)S(1)} %collective-permute-done.7.refs_2_) | copy-start | bytes 393220
  82.7 0.6 copy-start.10

commit v3 on v2

--- a/solution.py
+++ b/solution.py
@@ -9,7 +9,7 @@
 
 BLK = 128
 SOFTENING = 0.5
-UNROLL = 4
+UNROLL = 8
 CHUNK = 32
 VMEM_BYTES = 56 * 1024 * 1024
 SLOPE = 1.1283737853323306
@@ -88,14 +88,14 @@
     )(positions, atom_type[None, :], krylov, order[None, :])
 
 
-def scatter_kernel(order_ref, krylov_ref, type_ref, hard_ref, *refs):
+def scatter_kernel(order_ref, krylov_ref, type_ref, hard_ref, valid_ref, *refs):
     parts, (out_ref, split_ref) = refs[:-2], refs[-2:]
     vecs, atoms = krylov_ref.shape
     groups = atoms // BLK
     chunk = 512
     total = parts[0][...]
-    for part in parts[1:]:
-        total = total + part[...].astype(jnp.float32)
+    for index, part in enumerate(parts[1:]):
+        total = total + jnp.where(valid_ref[index] > 0, part[...].astype(jnp.float32), 0.0)
     high = total.astype(jnp.bfloat16).astype(jnp.float32)
     split_ref[0:vecs] = high
     split_ref[vecs:] = total - high
@@ -129,12 +129,12 @@
         out_ref[:, lanes] = placed + hardness[:, lanes] * krylov_ref[:, lanes]
 
 
-def scattered(order, krylov, atom_type, type_hard, parts):
+def scattered(order, krylov, atom_type, type_hard, valid, parts):
     vecs, atoms = krylov.shape
     vmem = pl.BlockSpec(memory_space=pltpu.VMEM)
     return pl.pallas_call(
         scatter_kernel,
-        in_specs=[vmem] * 3 + [pl.BlockSpec(memory_space=pltpu.SMEM)] + [vmem] * len(parts),
+        in_specs=[vmem] * 3 + [pl.BlockSpec(memory_space=pltpu.SMEM)] * 2 + [vmem] * len(parts),
         out_specs=vmem,
         out_shape=jax.ShapeDtypeStruct((vecs, atoms), jnp.float32),
         scratch_shapes=[pltpu.VMEM((2 * vecs, atoms), jnp.float32)],
@@ -143,7 +143,7 @@
             flops=4 * vecs * atoms * atoms, bytes_accessed=24 * vecs * atoms, transcendentals=0
         ),
         name="scatter_atoms",
-    )(order[None, :], krylov, atom_type[None, :], type_hard, *parts)
+    )(order[None, :], krylov, atom_type[None, :], type_hard, valid, *parts)
 
 
 def lanes_of(block):
@@ -297,15 +297,67 @@
     )(left_ids, right_ids, count, table, *geometries, *vectors)
 
 
-def along_row(value, steps):
-    count = lax.axis_size("row")
-    first, last = max(0, -steps), min(count, count - steps)
-    return lax.ppermute(value, "row", [(source, source + steps) for source in range(first, last)])
-
-
-def along_col(value, steps):
-    count = lax.axis_size("col")
-    return lax.ppermute(value, "col", [(source, (source + steps) % count) for source in range(count)])
+def exchange_kernel(peers, toward, items, *refs):
+    count = len(peers) * items
+    sources, targets = refs[:count], refs[count : 2 * count]
+    send_sems, recv_sems = refs[2 * count :]
+    barrier = pltpu.get_barrier_semaphore()
+
+    def neighbour(axis, shift):
+        size, here = lax.axis_size(axis), lax.axis_index(axis)
+        there = here + shift
+        if axis == "col":
+            return {axis: lax.rem(there + size, size)}, there == there
+        return {axis: there}, (there >= 0) & (there < size)
+
+    expected = jnp.int32(0)
+    for axis, step in peers:
+        device, exists = neighbour(axis, -toward * step)
+
+        @pl.when(exists)
+        def _():
+            pl.semaphore_signal(barrier, inc=1, device_id=device, device_id_type=pl.DeviceIdType.MESH)
+
+        expected = expected + neighbour(axis, toward * step)[1].astype(jnp.int32)
+    pl.semaphore_wait(barrier, expected)
+
+    def copy_of(index):
+        axis, step = peers[index // items]
+        device, exists = neighbour(axis, toward * step)
+        copy = pltpu.make_async_remote_copy(
+            src_ref=sources[index],
+            dst_ref=targets[index],
+            send_sem=send_sems.at[index],
+            recv_sem=recv_sems.at[index],
+            device_id=device,
+            device_id_type=pl.DeviceIdType.MESH,
+        )
+        return copy, exists, neighbour(axis, -toward * step)[1]
+
+    for index in range(count):
+        copy, exists, _ = copy_of(index)
+        pl.when(exists)(copy.start)
+    for index in range(count):
+        copy, exists, arrives = copy_of(index)
+        pl.when(exists)(copy.wait_send)
+        pl.when(arrives)(copy.wait_recv)
+
+
+def exchanged(panels, peers, toward, collective_id):
+    items = len(panels[0])
+    flat = [item for panel in panels for item in panel]
+    moved = pl.pallas_call(
+        functools.partial(exchange_kernel, peers, toward, items),
+        in_specs=[pl.BlockSpec(memory_space=pl.ANY)] * len(flat),
+        out_specs=[pl.BlockSpec(memory_space=pl.ANY)] * len(flat),
+        out_shape=[jax.ShapeDtypeStruct(item.shape, item.dtype) for item in flat],
+        scratch_shapes=[pltpu.SemaphoreType.DMA((len(flat),)), pltpu.SemaphoreType.DMA((len(flat),))],
+        compiler_params=pltpu.CompilerParams(
+            collective_id=collective_id, has_side_effects=True, vmem_limit_bytes=VMEM_BYTES
+        ),
+        name="send_atoms" if collective_id == 0 else "return_sums",
+    )(*flat)
+    return [moved[first : first + items] for first in range(0, len(flat), items)]
 
 
 def on_device(
@@ -317,9 +369,9 @@
 
     col_devices = lax.axis_size("col")
     peers = [("col", step) for step in range(1, col_devices)] + [("row", 1), ("row", 2)]
-    moved = {"col": along_col, "row": along_row}
-    geometries = [geometry] + [moved[axis](geometry, -step) for axis, step in peers]
-    panels = [vectors] + [moved[axis](vectors, -step) for axis, step in peers]
+    arrived = exchanged([(geometry, vectors)] * len(peers), peers, -1, 0)
+    geometries = [geometry] + [panel[0] for panel in arrived]
+    panels = [vectors] + [panel[1] for panel in arrived]
 
     row_index = lax.axis_index("row")
     col_index = lax.axis_index("col")
@@ -336,8 +388,9 @@
     sums = pair_sums(
         geometries, panels, left_ids, right_ids, pair_count.reshape(1), table, col_devices * shard_blocks
     )
-    returned = [sums[0]] + [moved[axis](part, step) for (axis, step), part in zip(peers, sums[1:])]
-    return scattered(block_order, krylov, atom_type, type_hard, returned)
+    returned = [panel[0] for panel in exchanged([(part,) for part in sums[1:]], peers, 1, 1)]
+    valid = jnp.stack([jnp.int32(1) if axis == "col" else (row_index >= step).astype(jnp.int32) for axis, step in peers])
+    return scattered(block_order, krylov, atom_type, type_hard, valid, [sums[0]] + returned)
 
 
 def solution(mesh):

time: 90.3 us -> 78.8 us (0.87)
  starting transfers between devices: 28.7 us -> 0 us
  Pallas kernels: 48.8 us -> 74.1 us
  waiting for transfers between devices: 8.84 us -> 0 us
    ppermute x9 -> x0, starting transfers between devices: 28.7 us -> none  [the longest x6 23.3 us: along_row(): lax.ppermute(value, 'row', [(source, source + steps) for source in range(...]
    pallas_call x0 -> x2, Pallas kernels: none -> 25.2 us  [exchanged(): pl.pallas_call(functools.partial(exchange_kernel, peers, toward, items),...]
    ppermute x9 -> x0, waiting for transfers between devices: 8.84 us -> none  [the longest x6 5.12 us: along_row(): lax.ppermute(value, 'row', [(source, source + steps) for source in range(...]
  transfers between devices with their start and end apart: 9 -> 0, of which waited for: 4 -> 0; matrix products, arithmetic and copies ran while one was open for 1% -> 0% of each run, Pallas kernels for 0% -> 0%
where the time goes in v3:
time: 78.8 us; the launch traced here: 77.3 us
  Pallas kernels  74.1 us (94%)
  local copies, waits for them, and re-layouts  1.37 us (2%)
  other arithmetic  1.17 us (1%)
    pallas_call x1, Pallas kernels, pair_sums(): pl.pallas_call(functools.partial(pair_kernel, slabs, left_blocks), in_spe...  35.7 us
    pallas_call x2, Pallas kernels, exchanged(): pl.pallas_call(functools.partial(exchange_kernel, peers, toward, items),...  25.2 us
    pallas_call x1, Pallas kernels, gathered(): pl.pallas_call(gather_kernel, grid=(atoms // tile,), in_specs=[pl.BlockSp...  7.43 us
    pallas_call x1, Pallas kernels, scattered(): pl.pallas_call(scatter_kernel, in_specs=[vmem] * 3 + [pl.BlockSpec(memory...  5.84 us

profile of v3, /device:TPU:16, one launch (start us, length us, event | category | flops | bytes accessed | tf_op | source)
XLA Modules:
  0.0 77.3 jit_solution(13149099270751638939)
XLA Ops:
  0.7 0.6 add_convert_fusion.valid_ref
  1.2 0.0 copy-start.2
  1.2 0.0 copy-start.1
  1.2 0.0 copy-start
  1.2 0.6 copy-done.2
  1.9 0.0 copy-done.1
  1.9 0.0 copy-done
  1.9 0.6 fusion.4
  2.5 0.7 add.42.table_ref
  3.2 7.4 %gather_atoms.1 = (f32[8,4096]{1,0:T(8,128)}, bf16[16,4096]{1,0:T(8,128)(2,1)}) custom-call(f32[3,4096]{1,0:T(4,128)} %place_ref.1, s32[1,4096]{1,0:T(1,128)} %bitcast.12, f32[16,4096]{1,0:T(8,128)} %krylov_ref.3, s32[1,4096]{1,0:T(1,128)} %bitcast.10), custom_call_target="tpu_custom_call" | custom-call | flops 1073741824 | bytes 524288 | tf_op jit(solution)/shard_map/gather_atoms/pallas_call | solution.py:65
  10.6 12.3 %send_atoms.1 = (f32[8,4096]{1,0:T(8,128)}, bf16[16,4096]{1,0:T(8,128)(2,1)}, f32[8,4096]{1,0:T(8,128)}, bf16[16,4096]{1,0:T(8,128)(2,1)}, f32[8,4096]{1,0:T(8,128)}, /*index=5*/bf16[16,4096]{1,0:T(8,128)(2,1)}) custom-call(f32[8,4096]{1,0:T(8,128)} %get-tuple-element.20.refs_0_.refs_2_.refs_4_, ...), custom_call_target="tpu_custom_call" | custom-call | tf_op jit(solution)/shard_map/send_atoms/pallas_call | solution.py:349
  22.9 35.7 %pair_sums.1 = (f32[16,4096]{1,0:T(8,128)}, bf16[16,4096]{1,0:T(8,128)(2,1)}, bf16[16,4096]{1,0:T(8,128)(2,1)}, bf16[16,4096]{1,0:T(8,128)(2,1)}) custom-call(s32[512]{0:T(512)} %get-tuple-element.35.left_ids, s32[512]{0:T(512)} %get-tuple-element.36.right_ids, s32[1]{0:T(128)} %bitcast.7.count_ref, f32[8,128]{1,0:T(8,128)} %add.42.table_ref, ...), custom_call_target="tpu_custom_call" | custom-call | flops 3221225472 | bytes 1572864 | tf_op jit(solution)/shard_map/pair_sums/pallas_call | solution.py:275
  58.6 12.9 %return_sums.1 = (bf16[16,4096]{1,0:T(8,128)(2,1)}, bf16[16,4096]{1,0:T(8,128)(2,1)}, bf16[16,4096]{1,0:T(8,128)(2,1)}) custom-call(bf16[16,4096]{1,0:T(8,128)(2,1)} %get-tuple-element.29.refs_0_, bf16[16,4096]{1,0:T(8,128)(2,1)} %get-tuple-element.30.refs_1_, bf16[16,4096]{1,0:T(8,128)(2,1)} %get-tuple-element.31.refs_2_), custom_call_target="tpu_custom_call" | custom-call | tf_op jit(solution)/shard_map/return_sums/pallas_call | solution.py:349
  71.5 5.8 %scatter_atoms.1 = f32[16,4096]{1,0:T(8,128)} custom-call(s32[1,4096]{1,0:T(1,128)} %bitcast.11, f32[16,4096]{1,0:T(8,128)} %krylov_ref.3, s32[1,4096]{1,0:T(1,128)} %bitcast.13, f32[6]{0:T(128)} %hard_ref.1, s32[3]{0:T(128)} %add_convert_fusion.valid_ref, f32[16,4096]{1,0:T(8,128)} %get-tuple-element.28.refs_0_, ...), custom_call_target="tpu_custom_call" | custom-call | flops 1073741824 | bytes 1572864 | tf_op jit(solution)/shard_map/scatter_atoms/pallas_call | solution.py:135
  (1 shorter events, 0.0 us)
Async XLA Ops:
  1.2 0.7 copy-start.2
  1.2 0.7 copy-start.1
  1.2 0.7 copy-start

commit v4 on v3

--- a/solution.py
+++ b/solution.py
@@ -9,7 +9,7 @@
 
 BLK = 128
 SOFTENING = 0.5
-UNROLL = 8
+UNROLL = 16
 CHUNK = 32
 VMEM_BYTES = 56 * 1024 * 1024
 SLOPE = 1.1283737853323306
@@ -34,49 +34,46 @@
     vecs = krylov_ref.shape[0]
     groups = atoms // BLK
     rows = 16 + vecs
-    width = order_ref.shape[1]
-
-    @pl.when(pl.program_id(0) == 0)
-    def _():
-        high, mid, low = split3(place_ref[...])
-        kinds = type_ref[...].astype(jnp.float32)
-        empty = jnp.zeros((6, atoms), jnp.float32)
-        full = jnp.concatenate([high, mid, low, kinds, empty, krylov_ref[...]], axis=0).astype(jnp.bfloat16)
-        for group in range(groups):
-            stacked_ref[group * rows : (group + 1) * rows] = full[:, group * BLK : (group + 1) * BLK]
-
-    order = order_ref[...]
-    group_of, lane_of = order // BLK, order % BLK
+    width = 2 * BLK
+    together = 8
+    high, mid, low = split3(place_ref[...])
+    kinds = type_ref[...].astype(jnp.float32)
+    empty = jnp.zeros((6, atoms), jnp.float32)
+    full = jnp.concatenate([high, mid, low, kinds, empty, krylov_ref[...]], axis=0).astype(jnp.bfloat16)
+    for group in range(groups):
+        stacked_ref[group * rows : (group + 1) * rows] = full[:, group * BLK : (group + 1) * BLK]
     lane_ids = lax.broadcasted_iota(jnp.int32, (BLK, width), 0)
-    picked = (lane_ids == lane_of).astype(jnp.float32).astype(jnp.bfloat16)
-    total = jnp.zeros((rows, width), jnp.float32)
-    for group in range(groups):
-        here = jnp.dot(
-            stacked_ref[group * rows : (group + 1) * rows], picked, preferred_element_type=jnp.float32
-        )
-        total = jnp.where(group_of == group, here, total)
-    place = total[0:3] + total[3:6] + total[6:9]
-    geometry_ref[...] = jnp.concatenate([place, total[9:10], jnp.zeros((4, width), jnp.float32)], axis=0)
-    vectors_ref[...] = total[16:].astype(jnp.bfloat16)
-
-
-def gathered(positions, atom_type, krylov, order, tile=512):
+
+    def chunk_step(step, carry):
+        lanes = pl.ds(pl.multiple_of(step * width, width), width)
+        order = order_ref[:, lanes]
+        picked = (lane_ids == order % BLK).astype(jnp.float32).astype(jnp.bfloat16)
+        group_of = jnp.broadcast_to(order // BLK, (rows, width))
+        total = jnp.zeros((rows, width), jnp.float32)
+        for first in range(0, groups, together):
+            here = jnp.dot(
+                stacked_ref[first * rows : (first + together) * rows], picked, preferred_element_type=jnp.float32
+            )
+            for offset in range(together):
+                part = here[offset * rows : (offset + 1) * rows]
+                total = jnp.where(group_of == first + offset, part, total)
+        place = total[0:3] + total[3:6] + total[6:9]
+        geometry_ref[:, lanes] = jnp.concatenate([place, total[9:10]], axis=0)
+        vectors_ref[:, lanes] = total[16:].astype(jnp.bfloat16)
+        return carry
+
+    lax.fori_loop(0, atoms // width, chunk_step, 0, unroll=2)
+
+
+def gathered(positions, atom_type, krylov, order):
     vecs, atoms = krylov.shape
+    vmem = pl.BlockSpec(memory_space=pltpu.VMEM)
     return pl.pallas_call(
         gather_kernel,
-        grid=(atoms // tile,),
-        in_specs=[
-            pl.BlockSpec((3, atoms), lambda step: (0, 0)),
-            pl.BlockSpec((1, atoms), lambda step: (0, 0)),
-            pl.BlockSpec((vecs, atoms), lambda step: (0, 0)),
-            pl.BlockSpec((1, tile), lambda step: (0, step)),
-        ],
-        out_specs=[
-            pl.BlockSpec((8, tile), lambda step: (0, step)),
-            pl.BlockSpec((vecs, tile), lambda step: (0, step)),
-        ],
+        in_specs=[vmem] * 4,
+        out_specs=[vmem] * 2,
         out_shape=[
-            jax.ShapeDtypeStruct((8, atoms), jnp.float32),
+            jax.ShapeDtypeStruct((4, atoms), jnp.float32),
             jax.ShapeDtypeStruct((vecs, atoms), jnp.bfloat16),
         ],
         scratch_shapes=[pltpu.VMEM((atoms // BLK * (16 + vecs), BLK), jnp.bfloat16)],
@@ -92,7 +89,7 @@
     parts, (out_ref, split_ref) = refs[:-2], refs[-2:]
     vecs, atoms = krylov_ref.shape
     groups = atoms // BLK
-    chunk = 512
+    chunk = 1024
     total = parts[0][...]
     for index, part in enumerate(parts[1:]):
         total = total + jnp.where(valid_ref[index] > 0, part[...].astype(jnp.float32), 0.0)
@@ -150,17 +147,20 @@
     return pl.ds(pl.multiple_of(block * BLK, BLK), BLK)
 
 
-def pair_kernel(slabs, left_blocks, left_ids, right_ids, count_ref, table_ref, *refs):
+def pair_kernel(slabs, left_blocks, left_ids, right_ids, count_ref, width_ref, *refs):
     geo_refs, vec_refs = refs[:slabs], refs[slabs : 2 * slabs]
     out_refs = refs[2 * slabs : 3 * slabs]
     left_ref, origin_ref, geo_ref, mix_ref, vec_ref, acc_ref, both_ref, tile_ref = refs[3 * slabs :]
     atoms = geo_refs[0].shape[1]
     blocks = slabs * atoms // BLK
     row_id = lax.broadcasted_iota(jnp.int32, (8, BLK), 0)
-    type_width = table_ref[...]
+    type_width = jnp.ones((8, BLK), jnp.float32)
+    for kind in range(width_ref.shape[0]):
+        type_width = jnp.where(row_id == kind, width_ref[kind], type_width)
+    geo_ref[4:8] = jnp.zeros((4, geo_ref.shape[1]), jnp.float32)
 
     for slab in range(slabs):
-        geo_ref[:, slab * atoms : (slab + 1) * atoms] = geo_refs[slab][...]
+        geo_ref[0:4, slab * atoms : (slab + 1) * atoms] = geo_refs[slab][...]
         vec_ref[:, slab * atoms : (slab + 1) * atoms] = vec_refs[slab][...]
     acc_ref[...] = jnp.zeros_like(acc_ref)
 
@@ -197,7 +197,7 @@
 
     both_ref[...] = jnp.ones_like(both_ref)
     tile_ref[...] = jnp.zeros_like(tile_ref)
-    slots = left_ids.shape[0]
+    slots = left_ids.shape[1]
     live = count_ref[0]
     zero_side = jnp.zeros((48, BLK), jnp.bfloat16)
     zero_mix = jnp.zeros((32, BLK), jnp.bfloat16)
@@ -233,7 +233,7 @@
     def slot_ids(turn, offset):
         slot = turn * UNROLL + offset
         place = jnp.clip(slot, 0, slots - 1)
-        return left_ids[place], right_ids[place], (slot >= 0) & (slot < live)
+        return left_ids[0, place], right_ids[0, place], (slot >= 0) & (slot < live)
 
     def pair_step(turn, carry):
         done = []
@@ -265,7 +265,7 @@
         out_refs[slab][...] = acc_ref[:, slab * atoms : (slab + 1) * atoms].astype(out_refs[slab].dtype)
 
 
-def pair_sums(geometries, vectors, left_ids, right_ids, count, table, left_blocks):
+def pair_sums(geometries, vectors, left_ids, right_ids, count, type_width, left_blocks):
     slabs = len(geometries)
     atoms = geometries[0].shape[1]
     vecs = vectors[0].shape[0]
@@ -274,7 +274,7 @@
     kinds = [jnp.float32] + [jnp.bfloat16] * (slabs - 1)
     return pl.pallas_call(
         functools.partial(pair_kernel, slabs, left_blocks),
-        in_specs=[smem] * 3 + [vmem] * (1 + 2 * slabs),
+        in_specs=[smem] * 4 + [vmem] * (2 * slabs),
         out_specs=[vmem] * slabs,
         out_shape=[jax.ShapeDtypeStruct((vecs, atoms), kind) for kind in kinds],
         scratch_shapes=[
@@ -289,18 +289,18 @@
         ],
         compiler_params=pltpu.CompilerParams(vmem_limit_bytes=VMEM_BYTES),
         cost_estimate=pl.CostEstimate(
-            flops=left_ids.shape[0] * BLK * BLK * (4 * vecs + 320),
+            flops=left_ids.shape[1] * BLK * BLK * (4 * vecs + 320),
             bytes_accessed=slabs * atoms * (32 + 4 * vecs),
-            transcendentals=2 * left_ids.shape[0] * BLK * BLK,
+            transcendentals=2 * left_ids.shape[1] * BLK * BLK,
         ),
         name="pair_sums",
-    )(left_ids, right_ids, count, table, *geometries, *vectors)
-
-
-def exchange_kernel(peers, toward, items, *refs):
+    )(left_ids, right_ids, count, type_width, *geometries, *vectors)
+
+
+def exchange_kernel(peers, toward, items, meanwhile, *refs):
     count = len(peers) * items
-    sources, targets = refs[:count], refs[count : 2 * count]
-    send_sems, recv_sems = refs[2 * count :]
+    sources = refs[:count]
+    targets, (send_sems, recv_sems) = refs[-2 - count : -2], refs[-2:]
     barrier = pltpu.get_barrier_semaphore()
 
     def neighbour(axis, shift):
@@ -337,27 +337,42 @@
     for index in range(count):
         copy, exists, _ = copy_of(index)
         pl.when(exists)(copy.start)
+    if meanwhile is not None:
+        meanwhile(*refs[count : -2 - count])
     for index in range(count):
         copy, exists, arrives = copy_of(index)
         pl.when(exists)(copy.wait_send)
         pl.when(arrives)(copy.wait_recv)
 
 
-def exchanged(panels, peers, toward, collective_id):
+def slot_ids_kernel(shard_blocks, rows_ref, cols_ref, left_ref, right_ref):
+    col_devices = lax.axis_size("col")
+    rows, cols = rows_ref[...], cols_ref[...]
+    row_slab = (rows // shard_blocks + (col_devices - lax.axis_index("col"))) % col_devices
+    left_ref[...] = row_slab * shard_blocks + rows % shard_blocks
+    step = jnp.clip(cols // shard_blocks - lax.axis_index("row"), 0, 2)
+    right_slab = jnp.where(step == 0, 0, step + col_devices - 1)
+    right_ref[...] = right_slab * shard_blocks + cols % shard_blocks
+
+
+def exchanged(panels, peers, toward, collective_id, meanwhile=None, extras=(), extra_outs=()):
     items = len(panels[0])
     flat = [item for panel in panels for item in panel]
-    moved = pl.pallas_call(
-        functools.partial(exchange_kernel, peers, toward, items),
-        in_specs=[pl.BlockSpec(memory_space=pl.ANY)] * len(flat),
-        out_specs=[pl.BlockSpec(memory_space=pl.ANY)] * len(flat),
-        out_shape=[jax.ShapeDtypeStruct(item.shape, item.dtype) for item in flat],
+    vmem = pl.BlockSpec(memory_space=pltpu.VMEM)
+    results = pl.pallas_call(
+        functools.partial(exchange_kernel, peers, toward, items, meanwhile),
+        in_specs=[pl.BlockSpec(memory_space=pl.ANY)] * len(flat) + [vmem] * len(extras),
+        out_specs=[vmem] * len(extra_outs) + [pl.BlockSpec(memory_space=pl.ANY)] * len(flat),
+        out_shape=list(extra_outs) + [jax.ShapeDtypeStruct(item.shape, item.dtype) for item in flat],
         scratch_shapes=[pltpu.SemaphoreType.DMA((len(flat),)), pltpu.SemaphoreType.DMA((len(flat),))],
         compiler_params=pltpu.CompilerParams(
             collective_id=collective_id, has_side_effects=True, vmem_limit_bytes=VMEM_BYTES
         ),
         name="send_atoms" if collective_id == 0 else "return_sums",
-    )(*flat)
-    return [moved[first : first + items] for first in range(0, len(flat), items)]
+    )(*flat, *extras)
+    moved = results[len(extra_outs) :]
+    arrived = [moved[first : first + items] for first in range(0, len(flat), items)]
+    return arrived, results[: len(extra_outs)]
 
 
 def on_device(
@@ -369,28 +384,27 @@
 
     col_devices = lax.axis_size("col")
     peers = [("col", step) for step in range(1, col_devices)] + [("row", 1), ("row", 2)]
-    arrived = exchanged([(geometry, vectors)] * len(peers), peers, -1, 0)
+    rows_list = pair_rows.reshape(1, -1)
+    cols_list = pair_cols.reshape(1, -1)
+    ids = jax.ShapeDtypeStruct(rows_list.shape, jnp.int32)
+    arrived, (left_ids, right_ids) = exchanged(
+        [(geometry, vectors)] * len(peers),
+        peers,
+        -1,
+        0,
+        functools.partial(slot_ids_kernel, shard_blocks),
+        (rows_list, cols_list),
+        (ids, ids),
+    )
     geometries = [geometry] + [panel[0] for panel in arrived]
     panels = [vectors] + [panel[1] for panel in arrived]
-
+    sums = pair_sums(
+        geometries, panels, left_ids, right_ids, pair_count.reshape(1), type_width, col_devices * shard_blocks
+    )
+    returned, _ = exchanged([(part,) for part in sums[1:]], peers, 1, 1)
     row_index = lax.axis_index("row")
-    col_index = lax.axis_index("col")
-    rows_list = pair_rows.reshape(-1)
-    cols_list = pair_cols.reshape(-1)
-    row_slab = (rows_list // shard_blocks - col_index + col_devices) % col_devices
-    left_ids = row_slab * shard_blocks + rows_list % shard_blocks
-    step = jnp.clip(cols_list // shard_blocks - row_index, 0, 2)
-    right_slab = jnp.where(step == 0, 0, step + col_devices - 1)
-    right_ids = right_slab * shard_blocks + cols_list % shard_blocks
-    table = jnp.zeros((8, BLK), jnp.float32) + jnp.pad(
-        type_width, (0, 8 - type_width.shape[0]), constant_values=1.0
-    )[:, None]
-    sums = pair_sums(
-        geometries, panels, left_ids, right_ids, pair_count.reshape(1), table, col_devices * shard_blocks
-    )
-    returned = [panel[0] for panel in exchanged([(part,) for part in sums[1:]], peers, 1, 1)]
     valid = jnp.stack([jnp.int32(1) if axis == "col" else (row_index >= step).astype(jnp.int32) for axis, step in peers])
-    return scattered(block_order, krylov, atom_type, type_hard, valid, [sums[0]] + returned)
+    return scattered(block_order, krylov, atom_type, type_hard, valid, [sums[0]] + [panel[0] for panel in returned])
 
 
 def solution(mesh):

time: 78.8 us -> 69.8 us (0.89)
  the two profiles are of different devices: /device:TPU:16 before, /device:TPU:0 now
where the time goes in v4:
time: 69.8 us; the launch traced here: 70 us
  Pallas kernels  68.7 us (98%)
    pallas_call x2, Pallas kernels, exchanged(): pl.pallas_call(functools.partial(exchange_kernel, peers, toward, items, m...  36.8 us
    pallas_call x1, Pallas kernels, pair_sums(): pl.pallas_call(functools.partial(pair_kernel, slabs, left_blocks), in_spe...  21.5 us
    pallas_call x1, Pallas kernels, gathered(): pl.pallas_call(gather_kernel, in_specs=[vmem] * 4, out_specs=[vmem] * 2,...  5.26 us
    pallas_call x1, Pallas kernels, scattered(): pl.pallas_call(scatter_kernel, in_specs=[vmem] * 3 + [pl.BlockSpec(memory...  5.12 us

profile of v4, /device:TPU:0, one launch (start us, length us, event | category | flops | bytes accessed | tf_op | source)
XLA Modules:
  0.0 70.0 jit_solution(4541765677466267882)
XLA Ops:
  0.0 5.3 %gather_atoms.1 = (f32[4,4096]{1,0:T(4,128)}, bf16[16,4096]{1,0:T(8,128)(2,1)}) custom-call(f32[3,4096]{1,0:T(4,128)} %place_ref.1, s32[1,4096]{1,0:T(1,128)} %bitcast.12, f32[16,4096]{1,0:T(8,128)} %krylov_ref.3, s32[1,4096]{1,0:T(1,128)} %bitcast.10), custom_call_target="tpu_custom_call" | custom-call | flops 1073741824 | bytes 524288 | tf_op jit(solution)/shard_map/gather_atoms/pallas_call | solution.py:71
  5.3 12.9 %send_atoms.1 = (s32[1,512]{1,0:T(1,128)}, s32[1,512]{1,0:T(1,128)}, f32[4,4096]{1,0:T(4,128)}, bf16[16,4096]{1,0:T(8,128)(2,1)}, f32[4,4096]{1,0:T(4,128)}, /*i...) custom-call(f32[4,4096]{1,0:T(4,128)} %get-tuple-element.22.refs_0_.refs_2_.refs_4_, ...), custom_call_target="tpu_custom_call" | custom-call | tf_op jit(solution)/shard_map/send_atoms/pallas_call | solution.py:362
  18.8 21.5 %pair_sums.1 = (f32[16,4096]{1,0:T(8,128)}, bf16[16,4096]{1,0:T(8,128)(2,1)}, bf16[16,4096]{1,0:T(8,128)(2,1)}, bf16[16,4096]{1,0:T(8,128)(2,1)}) custom-call(s32[1,512]{1,0:T(1,128)} %get-tuple-element.24.left_ids, s32[1,512]{1,0:T(1,128)} %get-tuple-element.25.right_ids, s32[1]{0:T(128)} %bitcast.7.count_ref, f32[6]{0:T(128)} %width_ref.1, ...), custom_call_target="tpu_custom_call" | custom-call | flops 3221225472 | bytes 1572864 | tf_op jit(solution)/shard_map/pair_sums/pallas_call | solution.py:275
  40.4 23.9 %return_sums.1 = (bf16[16,4096]{1,0:T(8,128)(2,1)}, bf16[16,4096]{1,0:T(8,128)(2,1)}, bf16[16,4096]{1,0:T(8,128)(2,1)}) custom-call(bf16[16,4096]{1,0:T(8,128)(2,1)} %get-tuple-element.33.refs_0_, bf16[16,4096]{1,0:T(8,128)(2,1)} %get-tuple-element.34.refs_1_, bf16[16,4096]{1,0:T(8,128)(2,1)} %get-tuple-element.35.refs_2_), custom_call_target="tpu_custom_call" | custom-call | tf_op jit(solution)/shard_map/return_sums/pallas_call | solution.py:362
  64.2 0.7 add_convert_fusion.valid_ref
  64.9 5.1 %scatter_atoms.1 = f32[16,4096]{1,0:T(8,128)} custom-call(s32[1,4096]{1,0:T(1,128)} %bitcast.11, f32[16,4096]{1,0:T(8,128)} %krylov_ref.3, s32[1,4096]{1,0:T(1,128)} %bitcast.13, f32[6]{0:T(128)} %hard_ref.1, s32[3]{0:T(128)} %add_convert_fusion.valid_ref, f32[16,4096]{1,0:T(8,128)} %get-tuple-element.32.refs_0_, ...), custom_call_target="tpu_custom_call" | custom-call | flops 1073741824 | bytes 1572864 | tf_op jit(solution)/shard_map/scatter_atoms/pallas_call | solution.py:132

commit v5 on v4

--- a/solution.py
+++ b/solution.py
@@ -92,7 +92,7 @@
     chunk = 1024
     total = parts[0][...]
     for index, part in enumerate(parts[1:]):
-        total = total + jnp.where(valid_ref[index] > 0, part[...].astype(jnp.float32), 0.0)
+        total = total + jnp.where(valid_ref[0, index] > 0, part[...].astype(jnp.float32), 0.0)
     high = total.astype(jnp.bfloat16).astype(jnp.float32)
     split_ref[0:vecs] = high
     split_ref[vecs:] = total - high
@@ -222,13 +222,12 @@
 
     def screened(square, inverse_width):
         inverse = lax.rsqrt(square)
-        scaled = square * inverse * inverse_width
-        narrow = scaled.astype(jnp.bfloat16)
+        narrow = square * inverse * inverse_width
         power = narrow * narrow
         series = jnp.bfloat16(ERF_SERIES[-1])
         for factor in ERF_SERIES[-2::-1] + (1.0,):
             series = series * power + jnp.bfloat16(factor)
-        return (jnp.tanh(narrow * series).astype(jnp.float32) * inverse).astype(jnp.bfloat16)
+        return jnp.tanh(narrow * series) * inverse
 
     def slot_ids(turn, offset):
         slot = turn * UNROLL + offset
@@ -253,7 +252,7 @@
             left, right, _ = slot_ids(turn, offset)
             both_ref[offset] = jnp.dot(
                 left_ref[left], weights_of(left, right), preferred_element_type=jnp.float32
-            )
+            ).astype(jnp.bfloat16)
         for left, right, forward, backward, alive in done:
             acc_ref[:, lanes_of(left)] += jnp.where(alive, forward, 0.0)
             acc_ref[:, lanes_of(right)] += jnp.where(alive & (left != right), backward, 0.0)
@@ -284,7 +283,7 @@
             pltpu.VMEM((32, slabs * atoms), jnp.bfloat16),
             pltpu.VMEM((vecs, slabs * atoms), jnp.bfloat16),
             pltpu.VMEM((vecs, slabs * atoms), jnp.float32),
-            pltpu.VMEM((UNROLL, BLK, 2 * BLK), jnp.float32),
+            pltpu.VMEM((UNROLL, BLK, 2 * BLK), jnp.bfloat16),
             pltpu.VMEM((UNROLL, BLK, BLK), jnp.bfloat16),
         ],
         compiler_params=pltpu.CompilerParams(vmem_limit_bytes=VMEM_BYTES),
@@ -345,7 +344,7 @@
         pl.when(arrives)(copy.wait_recv)
 
 
-def slot_ids_kernel(shard_blocks, rows_ref, cols_ref, left_ref, right_ref):
+def slot_ids_kernel(shard_blocks, peers, rows_ref, cols_ref, left_ref, right_ref, valid_ref):
     col_devices = lax.axis_size("col")
     rows, cols = rows_ref[...], cols_ref[...]
     row_slab = (rows // shard_blocks + (col_devices - lax.axis_index("col"))) % col_devices
@@ -353,6 +352,12 @@
     step = jnp.clip(cols // shard_blocks - lax.axis_index("row"), 0, 2)
     right_slab = jnp.where(step == 0, 0, step + col_devices - 1)
     right_ref[...] = right_slab * shard_blocks + cols % shard_blocks
+    place = lax.broadcasted_iota(jnp.int32, valid_ref.shape, 1)
+    valid = jnp.ones(valid_ref.shape, jnp.int32)
+    for index, (axis, shift) in enumerate(peers):
+        if axis == "row":
+            valid = jnp.where(place == index, (lax.axis_index("row") >= shift).astype(jnp.int32), valid)
+    valid_ref[...] = valid
 
 
 def exchanged(panels, peers, toward, collective_id, meanwhile=None, extras=(), extra_outs=()):
@@ -387,14 +392,14 @@
     rows_list = pair_rows.reshape(1, -1)
     cols_list = pair_cols.reshape(1, -1)
     ids = jax.ShapeDtypeStruct(rows_list.shape, jnp.int32)
-    arrived, (left_ids, right_ids) = exchanged(
+    arrived, (left_ids, right_ids, valid) = exchanged(
         [(geometry, vectors)] * len(peers),
         peers,
         -1,
         0,
-        functools.partial(slot_ids_kernel, shard_blocks),
+        functools.partial(slot_ids_kernel, shard_blocks, peers),
         (rows_list, cols_list),
-        (ids, ids),
+        (ids, ids, jax.ShapeDtypeStruct((1, BLK), jnp.int32)),
     )
     geometries = [geometry] + [panel[0] for panel in arrived]
     panels = [vectors] + [panel[1] for panel in arrived]
@@ -402,8 +407,6 @@
         geometries, panels, left_ids, right_ids, pair_count.reshape(1), type_width, col_devices * shard_blocks
     )
     returned, _ = exchanged([(part,) for part in sums[1:]], peers, 1, 1)
-    row_index = lax.axis_index("row")
-    valid = jnp.stack([jnp.int32(1) if axis == "col" else (row_index >= step).astype(jnp.int32) for axis, step in peers])
     return scattered(block_order, krylov, atom_type, type_hard, valid, [sums[0]] + [panel[0] for panel in returned])
 
 

time: 69.8 us -> 77.5 us (1.11)
  the two profiles are of different devices: /device:TPU:0 before, /device:TPU:25 now
where the time goes in v5:
time: 77.5 us; the launch traced here: 78.1 us
  Pallas kernels  77.4 us (100%)
    pallas_call x1, Pallas kernels, pair_sums(): pl.pallas_call(functools.partial(pair_kernel, slabs, left_blocks), in_spe...  40 us
    pallas_call x2, Pallas kernels, exchanged(): pl.pallas_call(functools.partial(exchange_kernel, peers, toward, items, m...  27 us
    pallas_call x1, Pallas kernels, gathered(): pl.pallas_call(gather_kernel, in_specs=[vmem] * 4, out_specs=[vmem] * 2,...  5.27 us
    pallas_call x1, Pallas kernels, scattered(): pl.pallas_call(scatter_kernel, in_specs=[vmem] * 3 + [pl.BlockSpec(memory...  5.12 us

profile of v5, /device:TPU:25, one launch (start us, length us, event | category | flops | bytes accessed | tf_op | source)
XLA Modules:
  0.0 78.1 jit_solution(6244931546151274032)
XLA Ops:
  0.7 5.3 %gather_atoms.1 = (f32[4,4096]{1,0:T(4,128)}, bf16[16,4096]{1,0:T(8,128)(2,1)}) custom-call(f32[3,4096]{1,0:T(4,128)} %place_ref.1, s32[1,4096]{1,0:T(1,128)} %bitcast.10, f32[16,4096]{1,0:T(8,128)} %krylov_ref.3, s32[1,4096]{1,0:T(1,128)} %bitcast.8), custom_call_target="tpu_custom_call" | custom-call | flops 1073741824 | bytes 524288 | tf_op jit(solution)/shard_map/gather_atoms/pallas_call | solution.py:71
  5.9 9.5 %send_atoms.1 = (s32[1,512]{1,0:T(1,128)}, s32[1,512]{1,0:T(1,128)}, s32[1,128]{1,0:T(1,128)}, f32[4,4096]{1,0:T(4,128)}, bf16[16,4096]{1,0:T(8,128)(2,1)}, /*in...) custom-call(f32[4,4096]{1,0:T(4,128)} %get-tuple-element.23.refs_0_.refs_2_.refs_4_, ...), custom_call_target="tpu_custom_call" | custom-call | tf_op jit(solution)/shard_map/send_atoms/pallas_call | solution.py:367
  15.5 40.0 %pair_sums.1 = (f32[16,4096]{1,0:T(8,128)}, bf16[16,4096]{1,0:T(8,128)(2,1)}, bf16[16,4096]{1,0:T(8,128)(2,1)}, bf16[16,4096]{1,0:T(8,128)(2,1)}) custom-call(s32[1,512]{1,0:T(1,128)} %get-tuple-element.26.left_ids, s32[1,512]{1,0:T(1,128)} %get-tuple-element.27.right_ids, s32[1]{0:T(128)} %bitcast.5.count_ref, f32[6]{0:T(128)} %width_ref.1, ...), custom_call_target="tpu_custom_call" | custom-call | flops 3221225472 | bytes 1572864 | tf_op jit(solution)/shard_map/pair_sums/pallas_call | solution.py:274
  55.5 17.5 %return_sums.1 = (bf16[16,4096]{1,0:T(8,128)(2,1)}, bf16[16,4096]{1,0:T(8,128)(2,1)}, bf16[16,4096]{1,0:T(8,128)(2,1)}) custom-call(bf16[16,4096]{1,0:T(8,128)(2,1)} %get-tuple-element.35.refs_0_, bf16[16,4096]{1,0:T(8,128)(2,1)} %get-tuple-element.36.refs_1_, bf16[16,4096]{1,0:T(8,128)(2,1)} %get-tuple-element.37.refs_2_), custom_call_target="tpu_custom_call" | custom-call | tf_op jit(solution)/shard_map/return_sums/pallas_call | solution.py:367
  73.0 5.1 %scatter_atoms.1 = f32[16,4096]{1,0:T(8,128)} custom-call(s32[1,4096]{1,0:T(1,128)} %bitcast.9, f32[16,4096]{1,0:T(8,128)} %krylov_ref.3, s32[1,4096]{1,0:T(1,128)} %bitcast.11, f32[6]{0:T(128)} %hard_ref.1, s32[1,128]{1,0:T(1,128)} %get-tuple-element.25.valid_ref, f32[16,4096]{1,0:T(8,128)} %get-tuple-element.34.refs_0_, ...), custom_call_target="tpu_custom_call" | custom-call | flops 1073741824 | bytes 1572864 | tf_op jit(solution)/shard_map/scatter_atoms/pallas_call | solution.py:132

commit v6 on v5

--- a/solution.py
+++ b/solution.py
@@ -195,8 +195,6 @@
 
     lax.fori_loop(0, left_blocks, left_step, 0, unroll=4)
 
-    both_ref[...] = jnp.ones_like(both_ref)
-    tile_ref[...] = jnp.zeros_like(tile_ref)
     slots = left_ids.shape[1]
     live = count_ref[0]
     zero_side = jnp.zeros((48, BLK), jnp.bfloat16)
@@ -222,21 +220,21 @@
 
     def screened(square, inverse_width):
         inverse = lax.rsqrt(square)
-        narrow = square * inverse * inverse_width
+        narrow = (square * inverse * inverse_width).astype(jnp.bfloat16)
         power = narrow * narrow
         series = jnp.bfloat16(ERF_SERIES[-1])
         for factor in ERF_SERIES[-2::-1] + (1.0,):
             series = series * power + jnp.bfloat16(factor)
-        return jnp.tanh(narrow * series) * inverse
+        return jnp.tanh(narrow * series) * inverse.astype(jnp.bfloat16)
 
     def slot_ids(turn, offset):
         slot = turn * UNROLL + offset
         place = jnp.clip(slot, 0, slots - 1)
         return left_ids[0, place], right_ids[0, place], (slot >= 0) & (slot < live)
 
-    def pair_step(turn, carry):
+    def pair_step(turn, products=True, tiles=True, starts=True):
         done = []
-        for offset in range(UNROLL):
+        for offset in range(UNROLL if products else 0):
             left, right, alive = slot_ids(turn - 2, offset)
             tile = tile_ref[offset]
             forward = lax.dot_general(
@@ -244,21 +242,29 @@
             )
             backward = jnp.dot(vec_ref[:, lanes_of(left)], tile, preferred_element_type=jnp.float32)
             done.append((left, right, forward, backward, alive))
-        for offset in range(UNROLL):
+        for offset in range(UNROLL if tiles else 0):
             for first in range(0, BLK, CHUNK):
                 rows = slice(first, first + CHUNK)
                 tile_ref[offset, rows] = screened(both_ref[offset, rows, :BLK], both_ref[offset, rows, BLK:])
-        for offset in range(UNROLL):
+        for offset in range(UNROLL if starts else 0):
             left, right, _ = slot_ids(turn, offset)
             both_ref[offset] = jnp.dot(
                 left_ref[left], weights_of(left, right), preferred_element_type=jnp.float32
-            ).astype(jnp.bfloat16)
+            )
         for left, right, forward, backward, alive in done:
             acc_ref[:, lanes_of(left)] += jnp.where(alive, forward, 0.0)
             acc_ref[:, lanes_of(right)] += jnp.where(alive & (left != right), backward, 0.0)
+
+    def full_step(turn, carry):
+        pair_step(turn)
         return carry
 
-    lax.fori_loop(0, (live + UNROLL - 1) // UNROLL + 2, pair_step, 0)
+    turns = jnp.maximum((live + UNROLL - 1) // UNROLL, 2)
+    pair_step(0, products=False, tiles=False)
+    pair_step(1, products=False)
+    lax.fori_loop(2, turns, full_step, 0)
+    pair_step(turns, starts=False)
+    pair_step(turns + 1, tiles=False, starts=False)
 
     for slab in range(slabs):
         out_refs[slab][...] = acc_ref[:, slab * atoms : (slab + 1) * atoms].astype(out_refs[slab].dtype)
@@ -283,7 +289,7 @@
             pltpu.VMEM((32, slabs * atoms), jnp.bfloat16),
             pltpu.VMEM((vecs, slabs * atoms), jnp.bfloat16),
             pltpu.VMEM((vecs, slabs * atoms), jnp.float32),
-            pltpu.VMEM((UNROLL, BLK, 2 * BLK), jnp.bfloat16),
+            pltpu.VMEM((UNROLL, BLK, 2 * BLK), jnp.float32),
             pltpu.VMEM((UNROLL, BLK, BLK), jnp.bfloat16),
         ],
         compiler_params=pltpu.CompilerParams(vmem_limit_bytes=VMEM_BYTES),

time: 77.5 us -> 66.6 us (0.86)
  the two profiles are of different devices: /device:TPU:25 before, /device:TPU:0 now
where the time goes in v6:
time: 66.6 us; the launch traced here: 65.9 us
  Pallas kernels  65.2 us (98%)
  between operations  0.67 us (1%)
    pallas_call x1, Pallas kernels, pair_sums(): pl.pallas_call(functools.partial(pair_kernel, slabs, left_blocks), in_spe...  28.9 us
    pallas_call x2, Pallas kernels, exchanged(): pl.pallas_call(functools.partial(exchange_kernel, peers, toward, items, m...  25.9 us
    pallas_call x1, Pallas kernels, gathered(): pl.pallas_call(gather_kernel, in_specs=[vmem] * 4, out_specs=[vmem] * 2,...  5.26 us
    pallas_call x1, Pallas kernels, scattered(): pl.pallas_call(scatter_kernel, in_specs=[vmem] * 3 + [pl.BlockSpec(memory...  5.12 us

profile of v6, /device:TPU:0, one launch (start us, length us, event | category | flops | bytes accessed | tf_op | source)
XLA Modules:
  0.0 65.9 jit_solution(2322629649441689097)
XLA Ops:
  0.7 5.3 %gather_atoms.1 = (f32[4,4096]{1,0:T(4,128)}, bf16[16,4096]{1,0:T(8,128)(2,1)}) custom-call(f32[3,4096]{1,0:T(4,128)} %place_ref.1, s32[1,4096]{1,0:T(1,128)} %bitcast.10, f32[16,4096]{1,0:T(8,128)} %krylov_ref.3, s32[1,4096]{1,0:T(1,128)} %bitcast.8), custom_call_target="tpu_custom_call" | custom-call | flops 1073741824 | bytes 524288 | tf_op jit(solution)/shard_map/gather_atoms/pallas_call | solution.py:71
  5.9 12.9 %send_atoms.1 = (s32[1,512]{1,0:T(1,128)}, s32[1,512]{1,0:T(1,128)}, s32[1,128]{1,0:T(1,128)}, f32[4,4096]{1,0:T(4,128)}, bf16[16,4096]{1,0:T(8,128)(2,1)}, /*in...) custom-call(f32[4,4096]{1,0:T(4,128)} %get-tuple-element.23.refs_0_.refs_2_.refs_4_, ...), custom_call_target="tpu_custom_call" | custom-call | tf_op jit(solution)/shard_map/send_atoms/pallas_call | solution.py:373
  18.8 28.9 %pair_sums.1 = (f32[16,4096]{1,0:T(8,128)}, bf16[16,4096]{1,0:T(8,128)(2,1)}, bf16[16,4096]{1,0:T(8,128)(2,1)}, bf16[16,4096]{1,0:T(8,128)(2,1)}) custom-call(s32[1,512]{1,0:T(1,128)} %get-tuple-element.26.left_ids, s32[1,512]{1,0:T(1,128)} %get-tuple-element.27.right_ids, s32[1]{0:T(128)} %bitcast.5.count_ref, f32[6]{0:T(128)} %width_ref.1, ...), custom_call_target="tpu_custom_call" | custom-call | flops 3221225472 | bytes 1572864 | tf_op jit(solution)/shard_map/pair_sums/pallas_call | solution.py:280
  47.8 13.0 %return_sums.1 = (bf16[16,4096]{1,0:T(8,128)(2,1)}, bf16[16,4096]{1,0:T(8,128)(2,1)}, bf16[16,4096]{1,0:T(8,128)(2,1)}) custom-call(bf16[16,4096]{1,0:T(8,128)(2,1)} %get-tuple-element.35.refs_0_, bf16[16,4096]{1,0:T(8,128)(2,1)} %get-tuple-element.36.refs_1_, bf16[16,4096]{1,0:T(8,128)(2,1)} %get-tuple-element.37.refs_2_), custom_call_target="tpu_custom_call" | custom-call | tf_op jit(solution)/shard_map/return_sums/pallas_call | solution.py:373
  60.7 5.1 %scatter_atoms.1 = f32[16,4096]{1,0:T(8,128)} custom-call(s32[1,4096]{1,0:T(1,128)} %bitcast.9, f32[16,4096]{1,0:T(8,128)} %krylov_ref.3, s32[1,4096]{1,0:T(1,128)} %bitcast.11, f32[6]{0:T(128)} %hard_ref.1, s32[1,128]{1,0:T(1,128)} %get-tuple-element.25.valid_ref, f32[16,4096]{1,0:T(8,128)} %get-tuple-element.34.refs_0_, ...), custom_call_target="tpu_custom_call" | custom-call | flops 1073741824 | bytes 1572864 | tf_op jit(solution)/shard_map/scatter_atoms/pallas_call | solution.py:132

commit v7 on v6

--- a/solution.py
+++ b/solution.py
@@ -302,7 +302,7 @@
     )(left_ids, right_ids, count, type_width, *geometries, *vectors)
 
 
-def exchange_kernel(peers, toward, items, meanwhile, *refs):
+def exchange_kernel(peers, toward, items, meanwhile, relay, *refs):
     count = len(peers) * items
     sources = refs[:count]
     targets, (send_sems, recv_sems) = refs[-2 - count : -2], refs[-2:]
@@ -315,39 +315,63 @@
             return {axis: lax.rem(there + size, size)}, there == there
         return {axis: there}, (there >= 0) & (there < size)
 
+    rows, row = lax.axis_size("row"), lax.axis_index("row")
+    even = lax.rem(row, 2) == 0
+    arriving = row + 2 < rows
+
+    def receiver(axis, step):
+        if relay and (axis, step) == ("row", 1):
+            return {axis: jnp.where(even, row + 1, row - 1)}, jnp.logical_not(even) | arriving
+        return neighbour(axis, toward * step)
+
+    def sender(axis, step):
+        if relay and (axis, step) == ("row", 1):
+            return {axis: jnp.where(even, row + 1, row - 1)}, even | (row + 1 < rows)
+        return neighbour(axis, -toward * step)
+
     expected = jnp.int32(0)
     for axis, step in peers:
-        device, exists = neighbour(axis, -toward * step)
+        device, exists = sender(axis, step)
 
         @pl.when(exists)
         def _():
             pl.semaphore_signal(barrier, inc=1, device_id=device, device_id_type=pl.DeviceIdType.MESH)
 
-        expected = expected + neighbour(axis, toward * step)[1].astype(jnp.int32)
+        expected = expected + receiver(axis, step)[1].astype(jnp.int32)
     pl.semaphore_wait(barrier, expected)
 
-    def copy_of(index):
-        axis, step = peers[index // items]
-        device, exists = neighbour(axis, toward * step)
+    def copy_of(index, source=None):
+        device, exists = receiver(*peers[index // items])
         copy = pltpu.make_async_remote_copy(
-            src_ref=sources[index],
+            src_ref=sources[index] if source is None else source,
             dst_ref=targets[index],
             send_sem=send_sems.at[index],
             recv_sem=recv_sems.at[index],
             device_id=device,
             device_id_type=pl.DeviceIdType.MESH,
         )
-        return copy, exists, neighbour(axis, -toward * step)[1]
-
-    for index in range(count):
+        return copy, exists, sender(*peers[index // items])[1]
+
+    relayed = [index for index in range(count) if relay and peers[index // items] == ("row", 1)]
+    for index in reversed(range(count)):
         copy, exists, _ = copy_of(index)
-        pl.when(exists)(copy.start)
+        pl.when(exists & jnp.logical_not(even) if index in relayed else exists)(copy.start)
     if meanwhile is not None:
         meanwhile(*refs[count : -2 - count])
+    for index in relayed:
+        first, _, arrives = copy_of(index + items)
+
+        @pl.when(arrives)
+        def _():
+            first.wait_recv()
+
+        onward, _, _ = copy_of(index, targets[index + items])
+        pl.when(even & arriving)(onward.start)
     for index in range(count):
         copy, exists, arrives = copy_of(index)
         pl.when(exists)(copy.wait_send)
-        pl.when(arrives)(copy.wait_recv)
+        if index - items not in relayed:
+            pl.when(arrives)(copy.wait_recv)
 
 
 def slot_ids_kernel(shard_blocks, peers, rows_ref, cols_ref, left_ref, right_ref, valid_ref):
@@ -366,12 +390,12 @@
     valid_ref[...] = valid
 
 
-def exchanged(panels, peers, toward, collective_id, meanwhile=None, extras=(), extra_outs=()):
+def exchanged(panels, peers, toward, collective_id, meanwhile=None, extras=(), extra_outs=(), relay=False):
     items = len(panels[0])
     flat = [item for panel in panels for item in panel]
     vmem = pl.BlockSpec(memory_space=pltpu.VMEM)
     results = pl.pallas_call(
-        functools.partial(exchange_kernel, peers, toward, items, meanwhile),
+        functools.partial(exchange_kernel, peers, toward, items, meanwhile, relay),
         in_specs=[pl.BlockSpec(memory_space=pl.ANY)] * len(flat) + [vmem] * len(extras),
         out_specs=[vmem] * len(extra_outs) + [pl.BlockSpec(memory_space=pl.ANY)] * len(flat),
         out_shape=list(extra_outs) + [jax.ShapeDtypeStruct(item.shape, item.dtype) for item in flat],
@@ -406,6 +430,7 @@
         functools.partial(slot_ids_kernel, shard_blocks, peers),
         (rows_list, cols_list),
         (ids, ids, jax.ShapeDtypeStruct((1, BLK), jnp.int32)),
+        relay=lax.axis_size("row") % 2 == 0,
     )
     geometries = [geometry] + [panel[0] for panel in arrived]
     panels = [vectors] + [panel[1] for panel in arrived]

time: 66.6 us -> 66.3 us (level)
  no operation moved by 1% of the time
where the time goes in v7:
time: 66.3 us; the launch traced here: 65.5 us
  Pallas kernels  64.9 us (98%)
  between operations  0.67 us (1%)
    pallas_call x1, Pallas kernels, pair_sums(): pl.pallas_call(functools.partial(pair_kernel, slabs, left_blocks), in_spe...  28.9 us
    pallas_call x2, Pallas kernels, exchanged(): pl.pallas_call(functools.partial(exchange_kernel, peers, toward, items, m...  25.6 us
    pallas_call x1, Pallas kernels, gathered(): pl.pallas_call(gather_kernel, in_specs=[vmem] * 4, out_specs=[vmem] * 2,...  5.26 us
    pallas_call x1, Pallas kernels, scattered(): pl.pallas_call(scatter_kernel, in_specs=[vmem] * 3 + [pl.BlockSpec(memory...  5.12 us

profile of v7, /device:TPU:0, one launch (start us, length us, event | category | flops | bytes accessed | tf_op | source)
XLA Modules:
  0.0 65.5 jit_solution(8527177776073073021)
XLA Ops:
  0.7 5.3 %gather_atoms.1 = (f32[4,4096]{1,0:T(4,128)}, bf16[16,4096]{1,0:T(8,128)(2,1)}) custom-call(f32[3,4096]{1,0:T(4,128)} %place_ref.1, s32[1,4096]{1,0:T(1,128)} %bitcast.10, f32[16,4096]{1,0:T(8,128)} %krylov_ref.3, s32[1,4096]{1,0:T(1,128)} %bitcast.8), custom_call_target="tpu_custom_call" | custom-call | flops 1073741824 | bytes 524288 | tf_op jit(solution)/shard_map/gather_atoms/pallas_call | solution.py:71
  5.9 12.2 %send_atoms.1 = (s32[1,512]{1,0:T(1,128)}, s32[1,512]{1,0:T(1,128)}, s32[1,128]{1,0:T(1,128)}, f32[4,4096]{1,0:T(4,128)}, bf16[16,4096]{1,0:T(8,128)(2,1)}, /*in...) custom-call(f32[4,4096]{1,0:T(4,128)} %get-tuple-element.23.refs_0_.refs_2_.refs_4_, ...), custom_call_target="tpu_custom_call" | custom-call | tf_op jit(solution)/shard_map/send_atoms/pallas_call | solution.py:397
  18.1 28.9 %pair_sums.1 = (f32[16,4096]{1,0:T(8,128)}, bf16[16,4096]{1,0:T(8,128)(2,1)}, bf16[16,4096]{1,0:T(8,128)(2,1)}, bf16[16,4096]{1,0:T(8,128)(2,1)}) custom-call(s32[1,512]{1,0:T(1,128)} %get-tuple-element.26.left_ids, s32[1,512]{1,0:T(1,128)} %get-tuple-element.27.right_ids, s32[1]{0:T(128)} %bitcast.5.count_ref, f32[6]{0:T(128)} %width_ref.1, ...), custom_call_target="tpu_custom_call" | custom-call | flops 3221225472 | bytes 1572864 | tf_op jit(solution)/shard_map/pair_sums/pallas_call | solution.py:280
  47.0 13.4 %return_sums.1 = (bf16[16,4096]{1,0:T(8,128)(2,1)}, bf16[16,4096]{1,0:T(8,128)(2,1)}, bf16[16,4096]{1,0:T(8,128)(2,1)}) custom-call(bf16[16,4096]{1,0:T(8,128)(2,1)} %get-tuple-element.35.refs_0_, bf16[16,4096]{1,0:T(8,128)(2,1)} %get-tuple-element.36.refs_1_, bf16[16,4096]{1,0:T(8,128)(2,1)} %get-tuple-element.37.refs_2_), custom_call_target="tpu_custom_call" | custom-call | tf_op jit(solution)/shard_map/return_sums/pallas_call | solution.py:397
  60.4 5.1 %scatter_atoms.1 = f32[16,4096]{1,0:T(8,128)} custom-call(s32[1,4096]{1,0:T(1,128)} %bitcast.9, f32[16,4096]{1,0:T(8,128)} %krylov_ref.3, s32[1,4096]{1,0:T(1,128)} %bitcast.11, f32[6]{0:T(128)} %hard_ref.1, s32[1,128]{1,0:T(1,128)} %get-tuple-element.25.valid_ref, f32[16,4096]{1,0:T(8,128)} %get-tuple-element.34.refs_0_, ...), custom_call_target="tpu_custom_call" | custom-call | flops 1073741824 | bytes 1572864 | tf_op jit(solution)/shard_map/scatter_atoms/pallas_call | solution.py:132
